TPU v7x, 256 devices: a whole 4x4x8 slice. The times are simulated.
256 devices in a mesh: section: 4 (over y_lo, core), batch: 16 (over z, y_hi), mp: 4 (over x).
Axes of the slice: x: 4, y: 4 (y_hi: 2, y_lo: 2; y = y_hi * 2 + y_lo), z: 8, core: 2. Of those that a mesh axis runs over, the one named last changes fastest.
Arguments:
- hidden_in: bfloat16 [1024, 8, 4096], P('batch'), may hold values from -6 to 6
- model_tokens: int32 [1024, 8, 8], P(('batch', 'section')), may hold values from 0 to 2047
- user_tokens: int32 [1024, 8, 8], P(('batch', 'section')), may hold values from 0 to 2047
- codebooks: bfloat16 [8, 2048, 256], P(None, 'batch'), may hold values from -2 to 2
- decode_proj: bfloat16 [256, 512], P(None, 'mp'), may hold values from -0.375 to 0.375
- conv_weight: bfloat16 [4, 3, 512, 512], P(None, None, None, 'mp'), may hold values from -0.21875 to 0.21875
- conv_state: bfloat16 [1024, 4, 2, 512], P(('batch', 'section')), may hold values from -0.8984375 to 2
- user_proj: bfloat16 [256, 4096], P(None, ('section', 'mp')), may hold values from -0.375 to 0.375
- norm_gain: bfloat16 [4096], replicated, may hold values from 0.5 to 1.5
- w_qkv: bfloat16 [4096, 3, 4096], P(None, None, ('section', 'mp')), as said below
- w_out: bfloat16 [4096, 4096], P(('section', 'mp')), may hold values from -0.375 to 0.375
- kv_cache: bfloat16 [2, 1024, 32, 64, 128], P(None, 'batch', ('section', 'mp')), may hold values from -6 to 6
- cache_len: int32 [1024], P('batch'), may hold values from 0 to 64, as said below
Outputs:
- layer_out: bfloat16 [1024, 8, 4096], P('batch')
- decoded: bfloat16 [1024, 8, 512], P(('batch', 'section'), None, 'mp')
Inputs may be any that keep to these rules, and one draw needn't show every extreme that they name: `cache_len`: a dialogue holds at most 64 earlier frames, and some dialogue holds exactly 64. `w_qkv`: every entry lies within 6 / sqrt(4096) of zero.
All inputs are finite; a program needn't handle non-finite values.
Results may differ from a plain program's by a relative error of at most 0.02.
Values may be sent and summed in bfloat16 or wider, within the bound.
A program may use at most 128 MiB of HBM per device.

v0:
```python
import jax
import jax.numpy as jnp
from jax import lax
from jax.sharding import PartitionSpec as P


def lookup(tokens, piece):
    count = piece.shape[1]
    picks = (tokens[:, :, None] == lax.broadcasted_iota(jnp.int32, (1, 1, count), 2)).astype(
        jnp.bfloat16
    )
    return jnp.einsum("rcn,cnd->rd", picks, piece, preferred_element_type=jnp.float32)


def rotate(x, pos):
    half = x.shape[-1] // 2
    freq = 10000.0 ** (-(jnp.arange(half, dtype=jnp.float32) * 2.0 / x.shape[-1]))
    angle = pos[..., None] * freq
    cosine = jnp.cos(angle)[..., None, :]
    sine = jnp.sin(angle)[..., None, :]
    first = x[..., :half]
    second = x[..., half:]
    return jnp.concatenate(
        [first * cosine - second * sine, first * sine + second * cosine], axis=-1
    )


def per_device(
    hidden_in,
    model_tokens,
    user_tokens,
    codebooks,
    decode_proj,
    conv_weight,
    conv_state,
    user_proj,
    norm_gain,
    w_qkv,
    w_out,
    kv_cache,
    cache_len,
):
    codec_dial, frames, books = model_tokens.shape
    codec_rows = codec_dial * frames
    both_tokens = jnp.concatenate(
        [model_tokens.reshape(codec_rows, books), user_tokens.reshape(codec_rows, books)], axis=0
    )
    latent = lookup(both_tokens, lax.all_gather(codebooks, "batch", axis=1, tiled=True))
    latent = latent.astype(jnp.bfloat16)
    latent_model = latent[:codec_rows]
    latent_user = latent[codec_rows:]
    group_latent = lax.all_gather(latent_user, "section", axis=0, tiled=True)
    emb_part = jnp.dot(group_latent, user_proj, preferred_element_type=jnp.float32).astype(
        jnp.bfloat16
    )
    user_emb = lax.all_gather(emb_part, ("section", "mp"), axis=1, tiled=True)
    group_dial, _, width = hidden_in.shape
    rows = group_dial * frames
    x0 = hidden_in.reshape(rows, width).astype(jnp.float32) + user_emb.astype(jnp.float32)
    meansq = jnp.mean(x0 * x0, axis=-1, keepdims=True)
    xn = (x0 * lax.rsqrt(meansq + 1e-05) * norm_gain.astype(jnp.float32)).astype(jnp.bfloat16)
    local_heads = kv_cache.shape[2]
    head_size = kv_cache.shape[4]
    slots = kv_cache.shape[3]
    qkv = jnp.dot(xn, w_qkv.reshape(width, -1), preferred_element_type=jnp.float32)
    qkv = qkv.reshape(group_dial, frames, 3, local_heads, head_size)
    pos = (cache_len[:, None] + jnp.arange(frames, dtype=jnp.int32)[None, :]).astype(jnp.float32)
    query = rotate(qkv[:, :, 0], pos).astype(jnp.bfloat16)
    key_new = rotate(qkv[:, :, 1], pos).astype(jnp.bfloat16)
    value_new = qkv[:, :, 2].astype(jnp.bfloat16)
    scale = 1.0 / head_size**0.5
    old_scores = (
        jnp.einsum("bfhe,bhce->bhfc", query, kv_cache[0], preferred_element_type=jnp.float32)
        * scale
    )
    valid = (jnp.arange(slots, dtype=jnp.int32)[None, :] < cache_len[:, None])[:, None, None, :]
    old_scores = jnp.where(valid, old_scores, -1e30)
    new_scores = (
        jnp.einsum("bfhe,bghe->bhfg", query, key_new, preferred_element_type=jnp.float32) * scale
    )
    causal = jnp.arange(frames)[None, :] <= jnp.arange(frames)[:, None]
    new_scores = jnp.where(causal[None, None], new_scores, -1e30)
    scores = jnp.concatenate([old_scores, new_scores], axis=-1)
    top = jnp.max(scores, axis=-1, keepdims=True)
    expo = jnp.exp(scores - top)
    probs = (expo / jnp.sum(expo, axis=-1, keepdims=True)).astype(jnp.bfloat16)
    attn = jnp.einsum(
        "bhfc,bhce->bfhe", probs[..., :slots], kv_cache[1], preferred_element_type=jnp.float32
    )
    attn = attn + jnp.einsum(
        "bhfg,bghe->bfhe", probs[..., slots:], value_new, preferred_element_type=jnp.float32
    )
    attn = attn.astype(jnp.bfloat16).reshape(rows, local_heads * head_size)
    proj = jnp.dot(attn, w_out, preferred_element_type=jnp.float32)
    total = lax.psum(proj.astype(jnp.bfloat16), ("section", "mp")).astype(jnp.float32)
    layer_out = (x0 + total).astype(jnp.bfloat16)
    layer_out = layer_out.reshape(group_dial, frames, width)
    state = jnp.dot(latent_model, decode_proj, preferred_element_type=jnp.float32).reshape(
        codec_dial, frames, -1
    )
    for layer in range(conv_weight.shape[0]):
        excited = jax.nn.elu(state).astype(jnp.bfloat16)
        full = lax.all_gather(excited, "mp", axis=2, tiled=True)
        padded = jnp.concatenate([conv_state[:, layer], full], axis=1)
        total_conv = state
        for tap in range(conv_weight.shape[1]):
            total_conv = total_conv + jnp.einsum(
                "dfc,co->dfo",
                padded[:, tap : tap + frames],
                conv_weight[layer, tap],
                preferred_element_type=jnp.float32,
            )
        state = total_conv
    decoded = state.astype(jnp.bfloat16)
    return (layer_out, decoded)


def solution(mesh):
    in_specs = (
        P("batch", None, None),
        P(("batch", "section"), None, None),
        P(("batch", "section"), None, None),
        P(None, "batch", None),
        P(None, "mp"),
        P(None, None, None, "mp"),
        P(("batch", "section"), None, None, None),
        P(None, ("section", "mp")),
        P(),
        P(None, None, ("section", "mp")),
        P(("section", "mp"), None),
        P(None, "batch", ("section", "mp"), None, None),
        P("batch"),
    )
    out_specs = (P("batch", None, None), P(("batch", "section"), None, "mp"))
    return jax.shard_map(
        per_device, mesh=mesh, in_specs=in_specs, out_specs=out_specs, check_vma=False
    )
```

profile of v0, /device:TPU:1, one launch (start us, length us, event | category | flops | bytes accessed | tf_op | source)
XLA Modules:
  0.0 399.4 jit_solution(16506816627993629476)
XLA Ops:
  8.9 0.8 copy.21
  9.9 140.0 %all-gather.3.cloned.1.call-done = bf16[8,2048,256]{2,1,0:T(8,128)(2,1)} async-done(((bf16[8,128,256]{2,1,0:T(8,128)(2,1)}), bf16[8,2048,256]{2,1,0:T(8,128)(2,1)}) %all-gather.3.cloned.1.call-update) | async-done | bytes 8388624 | tf_op jit(solution)/shard_map/all_gather | solution.py:48
  149.9 6.2 %fusion.29 = bf16[256,256]{1,0:T(8,128)(2,1)S(1)} fusion(bf16[8,2048,256]{2,1,0:T(8,128)(2,1)} %all-gather.3.cloned.1.call-done, s32[256,8]{0,1:T(8,128)S(1)} %pad_add_fusion), kind=kOutput, calls=%fused_computation.31 | convolution fusion | flops 2151743488 | bytes 8527872 | tf_op jit(solution)/shard_map/rcn,cnd->rd/dot_general | solution.py:12
  156.2 6.7 %all_gather.22 = bf16[512,256]{1,0:T(8,128)(2,1)S(1)} all-gather(bf16[128,256]{1,0:T(8,128)(2,1)S(1)} %slice.149), channel_id=1, replica_groups=mesh['section'=4,'batch'=16,'mp'=4] {'section'}, dimensions={0}, use_global_device_ids=true | all-gather | bytes 327680 | tf_op jit(solution)/shard_map/all_gather | solution.py:52
  162.9 0.9 convolution_convert_fusion.1
  164.1 8.7 %copy.22 = bf16[4096,3,256]{0,2,1:T(8,128)(2,1)} copy(bf16[4096,3,256]{2,0,1:T(8,128)(2,1)} %param.22) | data formatting | bytes 12582912 | tf_op args[9]
  173.0 1.0 multiply_cosine_fusion
  174.0 42.0 %all-gather.5.cloned.1.call-done = bf16[512,4096]{1,0:T(8,128)(2,1)} async-done(((bf16[512,256]{1,0:T(8,128)(2,1)}), bf16[512,4096]{1,0:T(8,128)(2,1)}) %all-gather.5.cloned.1.call-update) | async-done | bytes 4194320 | tf_op jit(solution)/shard_map/all_gather | solution.py:56
  216.0 5.0 %multiply_reduce_fusion = f32[512]{0:T(512)S(1)} fusion(bf16[512,4096]{1,0:T(8,128)(2,1)} %all-gather.5.cloned.1.call-done, bf16[64,8,4096]{2,1,0:T(8,128)(2,1)} %param.13), kind=kLoop, calls=%fused_computation.5 | loop fusion | flops 10485248 | bytes 8390656 | tf_op jit(solution)/shard_map/reduce_sum | solution.py:60
  221.0 0.9 copy-done.2
  221.9 6.7 %fusion.3 = f32[64,8,3,2,128]{4,1,3,2,0:T(8,128)S(1)} fusion(bf16[3,2,128,4096,1]{3,2,1,0,4:T(8,128)(2,1)} %bitcast.166, bf16[512,4096]{1,0:T(8,128)(2,1)S(1)} %copy-done.2, bf16[64,8,4096]{2,1,0:T(8,128)(2,1)S(1)} %copy-done.1, f32[4096]{0:T(1024)S(1)} %convert_element_type.70, f32[512]{0:T(512)S(1)} %add_rsqrt_fusion), kind=kOutput, calls=%fused_computation.9 | convolution fusion | flops 3233808384 | bytes 16271360 | tf_op jit(solution)/shard_map/dot_general | solution.py:65
  229.2 2.2 copy-done.3
  231.4 1.4 fusion.97
  235.1 4.6 %convolution_convert_fusion = bf16[512,4096]{1,0:T(8,128)(2,1)} fusion(bf16[256,4096]{1,0:T(8,128)(2,1)S(1)} %copy-done, f32[64,8,2,128]{3,1,2,0:T(8,128)S(1)} %fusion.15, f32[64,8,3,2,128]{4,1,3,2,0:T(8,128)} %copy-done.4, bf16[64,2,8,72]{3,2,1,0:T(8,128)(2,1)S(1)} %divide_convert_fusion), kind=kOutput, calls=%fused_computation.7 | convolution fusion | flops 1078198272 | bytes 7225344 | tf_op jit(solution)/shard_map/dot_general | solution.py:94
  240.1 8.9 %all_gather.24 = bf16[16,8,512]{2,1,0:T(8,128)(2,1)S(1)} all-gather(bf16[16,8,128]{2,1,0:T(8,128)(2,1)S(1)} %get-tuple-element.20), channel_id=1, replica_groups=mesh['section'=4,'batch'=16,'mp'=4] {'mp'}, dimensions={2}, use_global_device_ids=true | all-gather | bytes 163840 | tf_op jit(solution)/shard_map/all_gather | solution.py:103
  248.9 1.1 convolution_add_fusion.11
  250.0 1.1 convolution_add_fusion.10
  251.2 1.1 fusion.81
  252.3 9.7 %all_gather.25 = bf16[16,8,512]{2,1,0:T(8,128)(2,1)S(1)} all-gather(bf16[16,8,128]{2,1,0:T(8,128)(2,1)S(1)} %get-tuple-element.22), channel_id=1, replica_groups=mesh['section'=4,'batch'=16,'mp'=4] {'mp'}, dimensions={2}, use_global_device_ids=true | all-gather | bytes 163840 | tf_op jit(solution)/shard_map/all_gather | solution.py:103
  262.0 1.1 convolution_add_fusion.8
  263.1 1.1 convolution_add_fusion.7
  264.2 1.1 fusion.83
  265.3 10.3 %all_gather.26 = bf16[16,8,512]{2,1,0:T(8,128)(2,1)S(1)} all-gather(bf16[16,8,128]{2,1,0:T(8,128)(2,1)S(1)} %get-tuple-element.24), channel_id=1, replica_groups=mesh['section'=4,'batch'=16,'mp'=4] {'mp'}, dimensions={2}, use_global_device_ids=true | all-gather | bytes 163840 | tf_op jit(solution)/shard_map/all_gather | solution.py:103
  275.5 1.1 convolution_add_fusion.5
  276.6 1.1 convolution_add_fusion.4
  277.8 1.1 fusion.85
  278.9 10.2 %all_gather.27 = bf16[16,8,512]{2,1,0:T(8,128)(2,1)S(1)} all-gather(bf16[16,8,128]{2,1,0:T(8,128)(2,1)S(1)} %get-tuple-element.26), channel_id=1, replica_groups=mesh['section'=4,'batch'=16,'mp'=4] {'mp'}, dimensions={2}, use_global_device_ids=true | all-gather | bytes 163840 | tf_op jit(solution)/shard_map/all_gather | solution.py:103
  289.0 1.1 convolution_add_fusion.2
  290.1 1.1 convolution_add_fusion.1
  291.2 1.7 fusion.30
  292.9 90.5 %all-reduce.2.cloned.1.call-done = bf16[512,4096]{1,0:T(8,128)(2,1)} async-done(((bf16[512,4096]{1,0:T(8,128)(2,1)}), bf16[512,4096]{1,0:T(8,128)(2,1)}) %all-reduce.2.cloned.1.call-update) | async-done | bytes 4194320 | tf_op jit(solution)/shard_map/psum | solution.py:95
  383.4 9.5 %fusion.5 = bf16[64,8,4096]{2,1,0:T(8,128)(2,1)} fusion(bf16[512,4096]{1,0:T(8,128)(2,1)} %all-reduce.2.cloned.1.call-done, bf16[512,4096]{1,0:T(8,128)(2,1)} %all-gather.5.cloned.1.call-done, bf16[64,8,4096]{2,1,0:T(8,128)(2,1)} %param.13), kind=kLoop, calls=%fused_computation.10 | loop fusion | flops 12582912 | bytes 16777216 | tf_op jit(solution)/shard_map/reshape | solution.py:97
  (44 shorter events, 5.4 us)
Async XLA Ops:
  7.2 227.9 %copy-start = (bf16[256,4096]{1,0:T(8,128)(2,1)S(1)}, bf16[256,4096]{1,0:T(8,128)(2,1)}, u32[]{:S(2)}) copy-start(bf16[256,4096]{1,0:T(8,128)(2,1)} %param.23) | copy-start | bytes 6291460
  7.2 142.7 %all-gather.3.cloned.1.call-start = ((), (), s32[]{:S(2)}) async-start(), calls=%async_computation | async-start | bytes 8912896 | tf_op jit(solution)/shard_map/all_gather | solution.py:48
  7.9 208.1 %all-gather.5.cloned.1.call-start = ((), (), s32[]{:S(2)}) async-start(), calls=%async_computation.1 | async-start | bytes 4456448 | tf_op jit(solution)/shard_map/all_gather | solution.py:56
  9.8 153.0 %copy-start.5 = (bf16[256,256]{1,0:T(8,128)(2,1)S(1)}, bf16[256,256]{1,0:T(8,128)(2,1)}, u32[]{:S(2)}) copy-start(bf16[256,256]{1,0:T(8,128)(2,1)} %param.20) | copy-start | bytes 393220
  163.8 9.0 %copy-start.8 = (bf16[4096]{0:T(1024)(128)(2,1)S(1)}, bf16[4096]{0:T(1024)(128)(2,1)}, u32[]{:S(2)}) copy-start(bf16[4096]{0:T(1024)(128)(2,1)} %param.21) | copy-start | bytes 24580
  163.8 9.0 %copy-start.9 = (s32[64]{0:T(128)S(1)}, s32[64]{0:T(128)}, u32[]{:S(2)}) copy-start(s32[64]{0:T(128)} %param.25) | copy-start | bytes 772
  163.8 219.5 %all-reduce.2.cloned.1.call-start = ((), (), s32[]{:S(2)}) async-start(), calls=%async_computation.2 | async-start | bytes 8388608 | tf_op jit(solution)/shard_map/psum | solution.py:95
  216.0 5.0 %copy-start.1 = (bf16[64,8,4096]{2,1,0:T(8,128)(2,1)S(1)}, bf16[64,8,4096]{2,1,0:T(8,128)(2,1)}, u32[]{:S(2)}) copy-start(bf16[64,8,4096]{2,1,0:T(8,128)(2,1)} %param.13) | copy-start | bytes 12582916
  216.0 5.9 %copy-start.2 = (bf16[512,4096]{1,0:T(8,128)(2,1)S(1)}, bf16[512,4096]{1,0:T(8,128)(2,1)}, u32[]{:S(2)}) copy-start(bf16[512,4096]{1,0:T(8,128)(2,1)} %all-gather.5.cloned.1.call-done) | copy-start | bytes 12582916
  228.6 4.2 %copy-start.4 = (f32[64,8,3,2,128]{4,1,3,2,0:T(8,128)}, f32[64,8,3,2,128]{4,1,3,2,0:T(8,128)S(1)}, u32[]{:S(2)}) copy-start(f32[64,8,3,2,128]{4,1,3,2,0:T(8,128)S(1)} %fusion.3) | copy-start | bytes 4718596
  228.6 2.8 copy-start.3
  235.1 4.6 %copy-start.6 = (bf16[16,4,2,512]{3,2,1,0:T(2,128)(2,1)S(1)}, bf16[16,4,2,512]{3,2,1,0:T(2,128)(2,1)}, u32[]{:S(2)}) copy-start(bf16[16,4,2,512]{3,2,1,0:T(2,128)(2,1)} %param.19) | copy-start | bytes 393220
  235.1 4.8 %copy-start.7 = (bf16[256,128]{1,0:T(8,128)(2,1)S(1)}, bf16[256,128]{1,0:T(8,128)(2,1)}, u32[]{:S(2)}) copy-start(bf16[256,128]{1,0:T(8,128)(2,1)} %param.17) | copy-start | bytes 196612
Sparse Core Ops, SparseCore 0:
  10.6 139.2 all-gather.2
  163.9 51.9 all-gather.4
  239.9 143.4 all-reduce.1
where the time goes:
time: 400 us; the launch traced here: 399 us
  waiting for transfers between devices  273 us (68%)
  blocking collectives  45.7 us (11%)
  matrix products  35.1 us (9%)
  other arithmetic  17.2 us (4%)
  between operations  14 us (4%)
  local copies, waits for them, and re-layouts  13.8 us (3%)
    all_gather x1, waiting for transfers between devices, per_device(): lax.all_gather(codebooks, 'batch', axis=1, tiled=True)  140 us
    psum x1, waiting for transfers between devices, per_device(): lax.psum(proj.astype(jnp.bfloat16), ('section', 'mp')).astype(jnp.float32)  90.5 us
    all_gather x1, waiting for transfers between devices, per_device(): user_emb = lax.all_gather(emb_part, ('section', 'mp'), axis=1, tiled=True)  42 us
    all_gather x4, blocking collectives, per_device(): full = lax.all_gather(excited, 'mp', axis=2, tiled=True)  39 us
    dot_general x12, matrix products, per_device(): jnp.einsum('dfc,co->dfo', padded[:, tap:tap + frames], conv_weight[layer,...  13.8 us
    unnamed x23, local copies, waits for them, and re-layouts  13.5 us
    reshape x1, other arithmetic, per_device(): layer_out = layer_out.reshape(group_dial, frames, width)  9.46 us
  transfers between devices with their start and end apart: 3, of which 3 were waited for; matrix products, arithmetic and copies ran while one was open for 6% of the time, Pallas kernels for 0%

commit v1 on v0

v1 whole, which is shorter than its diff:
```python
import functools
import math

import jax
import jax.numpy as jnp
from jax import lax
from jax.experimental import pallas as pl
from jax.experimental.pallas import tpu as pltpu
from jax.sharding import PartitionSpec as P

F32 = jnp.float32
BF16 = jnp.bfloat16
MESH = pl.DeviceIdType.MESH

NS, NB, NM = 4, 16, 4
NG = NS * NM
ROWS = 512
WIDTH = 4096
NCHUNK = 4
CROWS = ROWS // NCHUNK
NEG = -1e30


def dot(a, b):
    return jnp.dot(a, b, preferred_element_type=F32)


def dot_t(a, b):
    return lax.dot_general(a, b, (((1,), (1,)), ((), ())), preferred_element_type=F32)


class Sems:
    def __init__(self, ref):
        self.ref = ref
        self.used = 0

    def take(self, count=1):
        first = self.used
        self.used += count
        return first


def kernel(
    h_hbm,
    mt_hbm,
    ut_hbm,
    cb_hbm,
    dp_hbm,
    cw_hbm,
    cs_hbm,
    up_hbm,
    g_hbm,
    w_hbm,
    wo_hbm,
    kv_hbm,
    len_ref,
    out_hbm,
    dec_hbm,
    h_v,
    tok_v,
    cb_v,
    dp_v,
    cw_v,
    el_v,
    g_v,
    w_v,
    wo_v,
    kv_v,
    upg,
    tsend,
    trecv,
    oh_u,
    oh_m,
    part_u,
    part_m,
    recv_u,
    recv_m,
    lg,
    lmg,
    lu,
    mq,
    mqb,
    acc,
    ss,
    cos_v,
    sin_v,
    attn_g,
    psend,
    precv,
    outv,
    decv,
    lsem,
    ssem,
    rsem,
):
    s = lax.axis_index("section")
    b = lax.axis_index("batch")
    m = lax.axis_index("mp")
    me = s * NM + m
    c1 = s + 1 - 2 * lax.rem(s, 2)
    y1 = lax.rem(s + 2, NS)
    xp = lax.rem(m + 1, NM)
    xm = lax.rem(m + NM - 1, NM)
    xd = lax.rem(m + 2, NM)

    local = Sems(lsem)
    remote = Sems(ssem)
    sends = []

    def load(src, dst):
        copy = pltpu.make_async_copy(src, dst, lsem.at[local.take()])
        copy.start()
        return copy

    def send(src, dst, ds=None, db=None, dm=None):
        at = remote.take()
        copy = pltpu.make_async_remote_copy(
            src_ref=src,
            dst_ref=dst,
            send_sem=ssem.at[at],
            recv_sem=rsem.at[at],
            device_id=(
                s if ds is None else ds,
                b if db is None else db,
                m if dm is None else dm,
            ),
            device_id_type=MESH,
        )
        copy.start()
        sends.append(copy)
        return copy

    def spread(src, dst, axis):
        base = remote.take(15)

        def make(k):
            if axis == "batch":
                target = lax.rem(b + k, NB)
                device = (s, target, m)
            else:
                target = lax.rem(me + k, NG)
                device = (target // NM, b, lax.rem(target, NM))
            return pltpu.make_async_remote_copy(
                src_ref=src(target),
                dst_ref=dst,
                send_sem=ssem.at[base + k - 1],
                recv_sem=rsem.at[base + k - 1],
                device_id=device,
                device_id_type=MESH,
            )

        @pl.loop(1, 16)
        def _(k):
            make(k).start()

        def wait_recv():
            @pl.loop(1, 16)
            def _(k):
                make(k).wait_recv()

        def wait_send():
            @pl.loop(1, 16)
            def _(k):
                make(k).wait_send()

        return wait_recv, wait_send

    l_ut = load(ut_hbm, tok_v.at[0])
    l_mt = load(mt_hbm, tok_v.at[1])
    l_g = load(g_hbm, g_v)
    l_cb = load(cb_hbm, cb_v)
    l_up = load(up_hbm, upg.at[me])
    l_h, l_w = [], []
    for part in range(4):
        cols = pl.ds(part * 1024, 1024)
        l_h.append(load(h_hbm.at[:, cols], h_v.at[:, cols]))
        l_w.append(load(w_hbm.at[:, cols], w_v.at[:, cols]))
    l_kv = load(kv_hbm, kv_v)
    own_cols = pl.ds(pl.multiple_of(s * 1024, 1024), 1024)
    l_wo = load(wo_hbm.at[:, own_cols], wo_v.at[s])
    l_dp = load(dp_hbm, dp_v)
    l_cw = load(cw_hbm, cw_v)
    l_cs = load(cs_hbm, el_v.at[:, pl.ds(0, 32)])

    barrier = pltpu.get_barrier_semaphore()

    @pl.loop(1, 16)
    def _(k):
        pl.semaphore_signal(
            barrier, inc=1, device_id=(s, lax.rem(b + k, NB), m), device_id_type=MESH
        )
        other = lax.rem(me + k, NG)
        pl.semaphore_signal(
            barrier, inc=1, device_id=(other // NM, b, lax.rem(other, NM)), device_id_type=MESH
        )

    pl.semaphore_wait(barrier, 30)

    l_ut.wait()
    l_mt.wait()
    f0 = 2 * m
    tile = jnp.concatenate(
        [
            tok_v[0, f0],
            tok_v[0, f0 + 1],
            tok_v[1, f0],
            tok_v[1, f0 + 1],
            jnp.zeros((8, 64), jnp.int32),
        ],
        axis=1,
    )
    tsend[...] = tile
    trecv[b] = tile
    tok_wait, tok_done = spread(lambda t: tsend, trecv.at[b], "batch")

    def up_block(block):
        return upg.at[block]

    l_up.wait()
    u_y = send(up_block(me), up_block(me), ds=y1)
    u_x = [send(up_block(me), up_block(me), dm=t) for t in (xp, xm, xd)]
    wo_copies = []
    for off in (1, 2, 3):
        if off == 1:
            target = c1
        elif off == 2:
            target = y1
        else:
            target = 3 - s
        cols = pl.ds(pl.multiple_of(target * 1024, 1024), 1024)
        wo_copies.append(send(wo_hbm.at[:, cols], wo_v.at[s], ds=target))

    l_g.wait()
    acc[...] = jnp.zeros_like(acc)

    def hidden_step(step):
        cols = pl.ds(pl.multiple_of(step * 512, 512), 512)
        scaled = (h_v[:, cols].astype(F32) * g_v[:, cols]).astype(BF16)
        for j in range(3):
            acc[j] += dot(scaled, w_v[j, cols, :])

    for part in range(2):
        l_h[part].wait()
        l_w[part].wait()
        pl.loop(2 * part, 2 * part + 2)(hidden_step)

    u_y.wait_recv()
    yblk = y1 * NM + m
    u_yx = [send(up_block(yblk), up_block(yblk), dm=t) for t in (xp, xm, xd)]

    tok_wait()
    l_cb.wait()
    entry = lax.broadcasted_iota(jnp.int32, (64, 128), 1) + 128 * b

    @pl.loop(0, NB)
    def _(i):
        rows = trecv[i].T[:64]
        start = pl.multiple_of(i * 32, 32)
        for c in range(8):
            hot = jnp.where(rows[:, c : c + 1] == entry, 1.0, 0.0).astype(BF16)
            oh_u[pl.ds(start, 32), pl.ds(c * 128, 128)] = hot[:32]
            oh_m[pl.ds(start, 32), pl.ds(c * 128, 128)] = hot[32:]

    part_u[...] = dot(oh_u[...], cb_v[...]).astype(BF16).reshape(NB, 32, 256)
    pu_wait, pu_done = spread(lambda t: part_u.at[t], recv_u.at[b], "batch")
    part_m[...] = dot(oh_m[...], cb_v[...]).astype(BF16).reshape(NB, 32, 256)
    pm_wait, pm_done = spread(lambda t: part_m.at[t], recv_m.at[b], "batch")
    recv_u[b] = part_u[b]
    recv_m[b] = part_m[b]

    for part in range(2, 4):
        l_h[part].wait()
        l_w[part].wait()
        pl.loop(2 * part, 2 * part + 2)(hidden_step)

    for copy in u_x + u_yx:
        copy.wait_recv()
    mine = pl.ds(pl.multiple_of(s * NM, NM), NM)
    yours = pl.ds(pl.multiple_of(y1 * NM, NM), NM)
    u_f0 = send(upg.at[mine], upg.at[mine], ds=c1)
    u_f1 = send(upg.at[yours], upg.at[yours], ds=c1)

    def total_of(ref):
        total = ref[0].astype(F32)
        for i in range(1, NB):
            total = total + ref[i].astype(F32)
        return total.astype(BF16)

    pu_wait()
    lg[me] = total_of(recv_u)
    lg_wait, lg_done = spread(lambda t: lg.at[me], lg.at[me], "group")

    lane = lax.broadcasted_iota(jnp.int32, (64, 128), 1)
    freq = jnp.exp(lax.rem(lane, 64).astype(F32) * (-2.0 * math.log(10000.0) / 128.0))
    frame = lax.rem(lax.broadcasted_iota(jnp.int32, (64, 128), 0), 8)

    @pl.loop(0, 8)
    def _(i):
        where = lax.broadcasted_iota(jnp.int32, (64, 128), 0) // 8
        pos = frame
        for d in range(8):
            pos = pos + jnp.where(where == d, len_ref[i * 8 + d], 0)
        angle = pos.astype(F32) * freq
        rows = pl.ds(pl.multiple_of(i * 64, 64), 64)
        cos_v[rows] = jnp.cos(angle)
        sine = jnp.sin(angle)
        sin_v[rows] = jnp.where(lane < 64, -sine, sine)

    pm_wait()
    lmg[m] = total_of(recv_m)
    lm_copies = [send(lmg.at[m], lmg.at[m], dm=t) for t in (xp, xm, xd)]

    mq[...] = jnp.zeros_like(mq)
    u_f0.wait_recv()
    u_f1.wait_recv()

    @pl.loop(0, NG)
    def _(j):
        cols = pl.ds(pl.multiple_of(j * 256, 256), 256)
        scaled = (upg[j].astype(F32) * g_v[:, cols]).astype(BF16)
        for t in range(3):
            mq[t] += dot(scaled, w_v[t, cols, :])

    mqb[...] = mq[...].astype(BF16)

    lg_wait()
    to = lax.broadcasted_iota(jnp.int32, (128, 128), 0)
    frm = lax.broadcasted_iota(jnp.int32, (128, 128), 1)
    perm = jnp.where(frm == lax.rem(to, 8) * 16 + to // 8, 1.0, 0.0).astype(BF16)
    perm_back = jnp.where(frm == lax.rem(to, 16) * 8 + to // 16, 1.0, 0.0).astype(BF16)
    for i in range(NS):
        group = lg[pl.ds(NM * i, NM)].reshape(128, 256)
        lu[pl.ds(128 * i, 128)] = dot(perm, group).astype(BF16)

    ss[...] = jnp.zeros_like(ss)

    @pl.loop(0, NG)
    def _(j):
        cols = pl.ds(pl.multiple_of(j * 256, 256), 256)
        x0 = h_v[:, cols].astype(F32) + dot(lu[...], upg[j])
        sq = x0 * x0
        ss[...] += sq[:, :128] + sq[:, 128:]

    l_kv.wait()
    my_cols = pl.ds(pl.multiple_of(me * 256, 256), 256)
    row8 = lax.broadcasted_iota(jnp.int32, (32, 32), 0)
    col8 = lax.broadcasted_iota(jnp.int32, (32, 32), 1)
    new_ok = (row8 // 8 == col8 // 8) & (lax.rem(col8, 8) <= lax.rem(row8, 8))
    slot = lax.broadcasted_iota(jnp.int32, (8, 256), 1)

    def attention(c):
        rows = pl.ds(c * CROWS, CROWS)
        r = lax.rsqrt(jnp.sum(ss[rows], axis=-1, keepdims=True) * (1.0 / WIDTH) + 1e-05)
        lat = lu[rows]
        q, k, v = [(acc[t, rows] + dot(lat, mqb[t])) * r for t in range(3)]
        cosine, sine = cos_v[rows], sin_v[rows]

        def rope(z):
            return (z * cosine + pltpu.roll(z, 64, 1) * sine).astype(BF16)

        for hd in range(2):
            cut = slice(128 * hd, 128 * hd + 128)
            qh, kh, vh = rope(q[:, cut]), rope(k[:, cut]), v[:, cut].astype(BF16)
            pieces = []
            for i in range(CROWS // 32):
                d0 = c * (CROWS // 8) + 4 * i
                sub = slice(32 * i, 32 * i + 32)
                keys = kv_v[0, pl.ds(d0, 4), hd].reshape(256, 128)
                values = kv_v[1, pl.ds(d0, 4), hd].reshape(256, 128)
                old = dot_t(qh[sub], keys) * (1.0 / math.sqrt(128.0))
                parts = []
                for d in range(4):
                    ok = (slot >= 64 * d) & (slot < 64 * d + len_ref[d0 + d])
                    parts.append(jnp.where(ok, old[8 * d : 8 * d + 8], NEG))
                old = jnp.concatenate(parts, axis=0)
                new = dot_t(qh[sub], kh[sub]) * (1.0 / math.sqrt(128.0))
                new = jnp.where(new_ok, new, NEG)
                top = jnp.maximum(
                    jnp.max(old, axis=-1, keepdims=True), jnp.max(new, axis=-1, keepdims=True)
                )
                old = jnp.exp(old - top)
                new = jnp.exp(new - top)
                total = jnp.sum(old, axis=-1, keepdims=True) + jnp.sum(
                    new, axis=-1, keepdims=True
                )
                mixed = dot(old.astype(BF16), values) + dot(new.astype(BF16), vh[sub])
                pieces.append((mixed / total).astype(BF16))
            attn_g[s, rows, pl.ds(128 * hd, 128)] = jnp.concatenate(pieces, axis=0)

    at = {}

    def stage_a(c):
        attention(c)
        rows = pl.ds(c * CROWS, CROWS)
        piece = attn_g.at[s, rows]
        at["t1", c] = send(piece, piece, ds=c1)
        at["t2", c] = send(piece, piece, ds=y1)

    def stage_f(c):
        at["t2", c].wait_recv()
        piece = attn_g.at[y1, pl.ds(c * CROWS, CROWS)]
        at["t3", c] = send(piece, piece, ds=c1)

    def stage_o(c):
        if c == 0:
            l_wo.wait()
            for copy in wo_copies:
                copy.wait_recv()
        at["t1", c].wait_recv()
        at["t3", c].wait_recv()
        rows = pl.ds(c * CROWS, CROWS)
        for t in range(NM):
            cols = pl.ds(256 * t, 256)
            proj = dot(attn_g[0, rows], wo_v[0, :, cols])
            for i in range(1, NS):
                proj = proj + dot(attn_g[i, rows], wo_v[i, :, cols])
            psend[t, rows] = proj.astype(BF16)
        at["p", c] = [
            send(psend.at[t, rows], precv.at[m, rows], dm=t) for t in (xp, xm, xd)
        ]

    def lanes(dst_s, dst_m, half):
        start = (dst_s * NM + dst_m) * 256 + 128 * half
        return pl.ds(pl.multiple_of(start, 128), 128)

    def piece_of(c, owner_s, owner_m, half, lower=0, count=CROWS):
        return outv.at[pl.ds(c * CROWS + lower, count), lanes(owner_s, owner_m, half)]

    def move(name, c, piece, **to):
        at[name, c] = send(piece, piece, **to)

    def stage_r(c):
        for copy in at["p", c]:
            copy.wait_recv()
        rows = pl.ds(c * CROWS, CROWS)
        total = psend[m, rows].astype(F32)
        for t in (xp, xm, xd):
            total = total + precv[t, rows].astype(F32)
        x0 = h_v[rows, my_cols].astype(F32) + dot(lu[rows], upg[me])
        outv[rows, my_cols] = (x0 + total).astype(BF16)
        own_a = piece_of(c, s, m, 0)
        own_b = piece_of(c, s, m, 1)
        move("a1", c, own_a, ds=y1)
        move("b1", c, own_b, dm=xp)
        move("b2", c, own_b, dm=xm)
        move("a2", c, own_a, dm=xp)
        move("a3", c, own_a, dm=xm)
        move("b3", c, own_b, ds=y1)

    def stage_g(c):
        half = CROWS // 2
        at["a1", c].wait_recv()
        ypiece = piece_of(c, y1, m, 0)
        move("a4", c, ypiece, dm=xp)
        move("a5", c, ypiece, dm=xm)
        at["b1", c].wait_recv()
        move("b4", c, piece_of(c, s, xm, 1, 0, half), dm=xp)
        move("b6", c, piece_of(c, s, xm, 1), ds=y1)
        at["b2", c].wait_recv()
        move("b5", c, piece_of(c, s, xp, 1, half, half), dm=xm)
        move("b7", c, piece_of(c, s, xp, 1), ds=y1)
        at["a2", c].wait_recv()
        move("a6", c, piece_of(c, s, xm, 0), dm=xp)

    def stage_h(c):
        half = CROWS // 2
        at["a4", c].wait_recv()
        at["a5", c].wait_recv()
        move("a7", c, piece_of(c, y1, xp, 0), dm=xm)
        at["b4", c].wait_recv()
        move("b8", c, piece_of(c, s, xd, 1, 0, half), ds=y1)
        at["b5", c].wait_recv()
        move("b9", c, piece_of(c, s, xd, 1, half, half), ds=y1)

    def stage_i(c):
        for name in ("a3", "a6", "a7", "b3", "b6", "b7", "b8", "b9"):
            at[name, c].wait_recv()
        rows = pl.ds(c * CROWS, CROWS)
        for name, owner in (("f1", s), ("f2", y1)):
            piece = outv.at[rows, pl.ds(pl.multiple_of(owner * 1024, 1024), 1024)]
            move(name, c, piece, ds=c1)

    stores = []

    def stage_j(c):
        at["f1", c].wait_recv()
        at["f2", c].wait_recv()
        rows = pl.ds(c * CROWS, CROWS)
        stores.append(load(outv.at[rows], out_hbm.at[rows]))

    codec = {}

    def codec_send(layer):
        state = codec["state"]
        excited = jnp.where(state > 0, state, jnp.exp(jnp.minimum(state, 0.0)) - 1.0)
        place = el_v.at[layer, pl.ds(32, 128), pl.ds(pl.multiple_of(m * 128, 128), 128)]
        place[...] = excited.astype(BF16)
        codec["copies"] = [send(place, place, dm=t) for t in (xp, xm, xd)]

    def codec_start():
        for copy in lm_copies:
            copy.wait_recv()
        l_dp.wait()
        l_cw.wait()
        l_cs.wait()
        codec["state"] = dot(lmg[...].reshape(128, 256), dp_v[...])
        codec_send(0)

    def codec_step(layer):
        for copy in codec["copies"]:
            copy.wait_recv()
        state = codec["state"]
        for tap in range(3):
            state = state + dot(el_v[layer, pl.ds(16 * tap, 128), :], cw_v[layer, tap])
        codec["state"] = state
        if layer < 3:
            codec_send(layer + 1)
        else:
            decv[...] = dot(perm, state.astype(BF16)).astype(BF16)
            stores.append(load(decv, dec_hbm))

    stages = [stage_a, stage_f, stage_o, stage_r, stage_g, stage_h, stage_i, stage_j]
    for step in range(NCHUNK + len(stages) - 1):
        if step == 1:
            codec_start()
        if 3 <= step <= 6:
            codec_step(step - 3)
        for depth in reversed(range(len(stages))):
            c = step - depth
            if 0 <= c < NCHUNK:
                stages[depth](c)

    for copy in sends:
        copy.wait_send()
    for done in (tok_done, pu_done, pm_done, lg_done):
        done()
    for copy in stores:
        copy.wait()


N_LOCAL = 32
N_REMOTE = 192


def per_device(
    hidden_in,
    model_tokens,
    user_tokens,
    codebooks,
    decode_proj,
    conv_weight,
    conv_state,
    user_proj,
    norm_gain,
    w_qkv,
    w_out,
    kv_cache,
    cache_len,
):
    any_space = pl.BlockSpec(memory_space=pl.ANY)
    smem = pl.BlockSpec(memory_space=pltpu.SMEM)
    vmem = pltpu.VMEM
    out, dec = pl.pallas_call(
        kernel,
        out_shape=(
            jax.ShapeDtypeStruct((ROWS, WIDTH), BF16),
            jax.ShapeDtypeStruct((128, 128), BF16),
        ),
        in_specs=[any_space] * 12 + [smem],
        out_specs=(any_space, any_space),
        scratch_shapes=[
            vmem((ROWS, WIDTH), BF16),
            vmem((2, 8, 8, 16), jnp.int32),
            vmem((1024, 256), BF16),
            vmem((256, 128), BF16),
            vmem((4, 3, 512, 128), BF16),
            vmem((4, 160, 512), BF16),
            vmem((1, WIDTH), F32),
            vmem((3, WIDTH, 256), BF16),
            vmem((NS, 256, 1024), BF16),
            vmem((2, 64, 2, 64, 128), BF16),
            vmem((NG, 256, 256), BF16),
            vmem((8, 128), jnp.int32),
            vmem((NB, 8, 128), jnp.int32),
            vmem((512, 1024), BF16),
            vmem((512, 1024), BF16),
            vmem((NB, 32, 256), BF16),
            vmem((NB, 32, 256), BF16),
            vmem((NB, 32, 256), BF16),
            vmem((NB, 32, 256), BF16),
            vmem((NG, 32, 256), BF16),
            vmem((NM, 32, 256), BF16),
            vmem((ROWS, 256), BF16),
            vmem((3, 256, 256), F32),
            vmem((3, 256, 256), BF16),
            vmem((3, ROWS, 256), F32),
            vmem((ROWS, 128), F32),
            vmem((ROWS, 128), F32),
            vmem((ROWS, 128), F32),
            vmem((NS, ROWS, 256), BF16),
            vmem((NM, ROWS, 256), BF16),
            vmem((NM, ROWS, 256), BF16),
            vmem((ROWS, WIDTH), BF16),
            vmem((128, 128), BF16),
            pltpu.SemaphoreType.DMA((N_LOCAL,)),
            pltpu.SemaphoreType.DMA((N_REMOTE,)),
            pltpu.SemaphoreType.DMA((N_REMOTE,)),
        ],
        compiler_params=pltpu.CompilerParams(
            collective_id=0, has_side_effects=True, vmem_limit_bytes=56 * 1024 * 1024
        ),
        cost_estimate=pl.CostEstimate(
            flops=12_000_000_000, bytes_accessed=30_000_000, transcendentals=1_000_000
        ),
    )(
        hidden_in.reshape(ROWS, WIDTH),
        jnp.transpose(model_tokens, (1, 2, 0)),
        jnp.transpose(user_tokens, (1, 2, 0)),
        codebooks.reshape(1024, 256),
        decode_proj,
        conv_weight,
        jnp.transpose(conv_state, (1, 2, 0, 3)).reshape(4, 32, 512),
        user_proj,
        norm_gain.astype(F32).reshape(1, WIDTH),
        jnp.transpose(w_qkv, (1, 0, 2)),
        w_out,
        kv_cache,
        cache_len,
    )
    return out.reshape(64, 8, WIDTH), dec.reshape(16, 8, 128)


def solution(mesh):
    in_specs = (
        P("batch", None, None),
        P(("batch", "section"), None, None),
        P(("batch", "section"), None, None),
        P(None, "batch", None),
        P(None, "mp"),
        P(None, None, None, "mp"),
        P(("batch", "section"), None, None, None),
        P(None, ("section", "mp")),
        P(),
        P(None, None, ("section", "mp")),
        P(("section", "mp"), None),
        P(None, "batch", ("section", "mp"), None, None),
        P("batch"),
    )
    out_specs = (P("batch", None, None), P(("batch", "section"), None, "mp"))
    return jax.shard_map(
        per_device, mesh=mesh, in_specs=in_specs, out_specs=out_specs, check_vma=False
    )
```

time: 400 us -> 118 us (0.29)
  waiting for transfers between devices: 273 us -> 0 us
  Pallas kernels: 0 us -> 108 us
  blocking collectives: 45.7 us -> 0 us
  matrix products: 35.1 us -> 0 us
  other arithmetic: 17.2 us -> 1.3 us
  between operations: 14 us -> 0.65 us
  local copies, waits for them, and re-layouts: 13.8 us -> 6.92 us
    all_gather x2 -> x0, waiting for transfers between devices: 182 us -> none  [the longest x1 140 us: per_device(): lax.all_gather(codebooks, 'batch', axis=1, tiled=True)]
    pallas_call x0 -> x1, Pallas kernels: none -> 108 us  [per_device(): pl.pallas_call(kernel, out_shape=(jax.ShapeDtypeStruct((ROWS, WIDTH), BF1...]
    psum x1 -> x0, waiting for transfers between devices: 90.5 us -> none  [per_device(): lax.psum(proj.astype(jnp.bfloat16), ('section', 'mp')).astype(jnp.float32)]
    all_gather x5 -> x0, blocking collectives: 45.7 us -> none  [the longest x4 39 us: per_device(): full = lax.all_gather(excited, 'mp', axis=2, tiled=True)]
    dot_general x20 -> x0, matrix products: 35.1 us -> none  [the longest x12 13.8 us: per_device(): jnp.einsum('dfc,co->dfo', padded[:, tap:tap + frames], conv_weight[layer,...]
    unnamed x23 -> x4, local copies, waits for them, and re-layouts: 13.5 us -> 5.32 us
    reshape x1, other arithmetic: 9.46 us -> 1.3 us  [per_device(): norm_gain.astype(F32).reshape(1, WIDTH)]
    reduce_sum x2 -> x0, other arithmetic: 5.6 us -> none  [the longest x1 5.03 us: per_device(): meansq = jnp.mean(x0 * x0, axis=-1, keepdims=True)]
  transfers between devices with their start and end apart: 3 -> 0, of which waited for: 3 -> 0; matrix products, arithmetic and copies ran while one was open for 6% -> 0% of each run, Pallas kernels for 0% -> 0%
where the time goes in v1:
time: 118 us; the launch traced here: 117 us
  Pallas kernels  108 us (92%)
  local copies, waits for them, and re-layouts  6.92 us (6%)
  other arithmetic  1.3 us (1%)
    pallas_call x1, Pallas kernels, per_device(): pl.pallas_call(kernel, out_shape=(jax.ShapeDtypeStruct((ROWS, WIDTH), BF1...  108 us
    unnamed x4, local copies, waits for them, and re-layouts  5.32 us

profile of v1, /device:TPU:1, one launch (start us, length us, event | category | flops | bytes accessed | tf_op | source)
XLA Modules:
  0.0 117.3 jit_solution(12856920259210642690)
XLA Ops:
  0.6 1.3 %reshape.31 = f32[4096]{0:T(1024)} convert(bf16[4096]{0:T(1024)(128)(2,1)} %param.21) | non-fusion elementwise | flops 4096 | bytes 24576 | tf_op jit(solution)/shard_map/reshape | solution.py:624
  1.9 1.6 %copy.15 = bf16[4,2,16,512]{3,2,1,0:T(8,128)(2,1)} copy(bf16[4,2,16,512]{3,1,0,2:T(2,128)(2,1)} %bitcast.11) | data formatting | bytes 262144 | tf_op jit(solution)/shard_map/transpose | solution.py:622
  3.5 108.5 %shard_map.140 = (bf16[512,4096]{1,0:T(8,128)(2,1)}, bf16[128,128]{1,0:T(8,128)(2,1)}) custom-call(bf16[512,4096]{1,0:T(8,128)(2,1)} %bitcast.16, s32[8,8,16]{2,1,0:T(8,128)} %bitcast.18, s32[8,8,16]{2,1,0:T(8,128)} %bitcast.19, bf16[1024,256]{1,0:T(8,128)(2,1)} %bitcast.17, bf16[256,128]{1,0:T(8,128)(2,1)} %dp_hbm.1, bf16[4,3,512,128]{3,2,1,0:T(8,128)(2,1)} %cw_hbm.1, ...), custom_call_target="tpu_custom_call" | custom-call | flops 12000000000 | bytes 30000000 | tf_op jit(solution)/shard_map/pallas_call | solution.py:563
  112.0 0.0 copy-start
  112.0 4.7 %copy.18 = bf16[64,8,4096]{2,1,0:T(8,128)(2,1)} copy(bf16[64,8,4096]{2,1,0:T(8,128)(2,1)} %bitcast.10) | data formatting | bytes 8388608
  116.7 0.0 copy-done
  116.7 0.6 copy.19
Async XLA Ops:
  112.0 4.7 %copy-start = (bf16[128,128]{1,0:T(8,128)(2,1)S(1)}, bf16[128,128]{1,0:T(8,128)(2,1)}, u32[]{:S(2)}) copy-start(bf16[128,128]{1,0:T(8,128)(2,1)} %get-tuple-element.5) | copy-start | bytes 98308

commit v2 on v1

v2 whole, which is shorter than its diff:
```python
import functools
import math

import jax
import jax.numpy as jnp
from jax import lax
from jax.experimental import pallas as pl
from jax.experimental.pallas import tpu as pltpu
from jax.sharding import PartitionSpec as P

F32 = jnp.float32
BF16 = jnp.bfloat16
MESH = pl.DeviceIdType.MESH

NS, NB, NM = 4, 16, 4
NG = NS * NM
ROWS = 512
WIDTH = 4096
NCHUNK = 4
CROWS = ROWS // NCHUNK
NEG = -1e30


def dot(a, b):
    return jnp.dot(a, b, preferred_element_type=F32)


def dot_t(a, b):
    return lax.dot_general(a, b, (((1,), (1,)), ((), ())), preferred_element_type=F32)


class Sems:
    def __init__(self):
        self.used = 0

    def take(self, count=1):
        first = self.used
        self.used += count
        return first


def kernel(
    h_hbm,
    mt_hbm,
    ut_hbm,
    cb_hbm,
    dp_hbm,
    cw_hbm,
    cs_hbm,
    up_hbm,
    g_hbm,
    w_hbm,
    wo_hbm,
    kv_hbm,
    len_ref,
    outv,
    decv,
    h_v,
    tok_v,
    cb_v,
    dp_v,
    cw_v,
    cs_v,
    el_v,
    st_v,
    g32_v,
    g_v,
    w_v,
    wo_v,
    kv_v,
    upg,
    tsend,
    trecv,
    tt,
    oh,
    part,
    recv,
    lg,
    lmg,
    lu,
    mq,
    mqb,
    acc,
    ss,
    cos_v,
    sin_v,
    attn_g,
    psend,
    ra_y,
    a2,
    rap,
    ram,
    a3p,
    a3m,
    ra2p,
    ra2m,
    rbp,
    rbm,
    b2p,
    b2m,
    rb2p,
    rb2m,
    b_own,
    b_y,
    rby,
    lsem,
    ssem,
    rsem,
):
    s = lax.axis_index("section")
    b = lax.axis_index("batch")
    m = lax.axis_index("mp")
    me = s * NM + m
    core = lax.rem(s, 2)
    y = s // 2
    c1 = s + 1 - 2 * core
    y1 = lax.rem(s + 2, NS)
    xp = lax.rem(m + 1, NM)
    xm = lax.rem(m + NM - 1, NM)
    xd = lax.rem(m + 2, NM)

    local = Sems()
    remote = Sems()
    finish = []

    def load(src, dst):
        copy = pltpu.make_async_copy(src, dst, lsem.at[local.take()])
        copy.start()
        return copy

    def remote_copy(src, dst, at, ds=None, db=None, dm=None):
        return pltpu.make_async_remote_copy(
            src_ref=src,
            dst_ref=dst,
            send_sem=ssem.at[at],
            recv_sem=rsem.at[at],
            device_id=(
                s if ds is None else ds,
                b if db is None else db,
                m if dm is None else dm,
            ),
            device_id_type=MESH,
        )

    def send(src, dst, **to):
        copy = remote_copy(src, dst, remote.take(), **to)
        copy.start()
        finish.append(copy.wait_send)
        return copy

    class Spread:
        def __init__(self, axis, src, dst, count=1):
            self.base = remote.take(15 * count)
            self.axis, self.src, self.dst, self.count = axis, src, dst, count
            finish.append(self.wait_send)

        def make(self, k, which):
            at = self.base + 15 * which + k - 1
            if self.axis == "batch":
                target = lax.rem(b + k, NB)
                return remote_copy(self.src(target, which), self.dst(which), at, db=target)
            target = lax.rem(me + k, NG)
            return remote_copy(
                self.src(target, which),
                self.dst(which),
                at,
                ds=target // NM,
                dm=lax.rem(target, NM),
            )

        def start(self, which=0):
            @pl.loop(1, 16)
            def _(k):
                self.make(k, which).start()

        def wait_recv(self, which=0):
            @pl.loop(1, 16)
            def _(k):
                self.make(k, which).wait_recv()

        def wait_send(self):
            for which in range(self.count):

                @pl.loop(1, 16)
                def _(k):
                    self.make(k, which).wait_send()

    class Event:
        def __init__(self, src, dst, count=NCHUNK, **to):
            self.base = remote.take(count)
            self.src, self.dst, self.to, self.count = src, dst, to, count
            finish.append(self.wait_sends)

        def make(self, c):
            return remote_copy(self.src(c), self.dst(c), self.base + c, **self.to)

        def start(self, c):
            self.make(c).start()

        def wait(self, c):
            self.make(c).wait_recv()

        def wait_sends(self):
            @pl.loop(0, self.count)
            def _(c):
                self.make(c).wait_send()

    l_ut = load(ut_hbm, tok_v.at[0])
    l_mt = load(mt_hbm, tok_v.at[1])
    l_up = load(up_hbm, upg.at[me])
    l_cb = load(cb_hbm, cb_v)
    l_g = load(g_hbm, g32_v)
    l_h = load(h_hbm, h_v)
    l_w = load(w_hbm, w_v)
    l_wo = []
    for yy in range(2):
        cols = pl.ds(pl.multiple_of((2 * yy + core) * 1024, 1024), 1024)
        l_wo.append(load(wo_hbm.at[:, cols], wo_v.at[core, yy]))
    l_cs = load(cs_hbm, cs_v)
    l_kv = load(kv_hbm, kv_v)
    l_dp = load(dp_hbm, dp_v)
    l_cw = load(cw_hbm, cw_v)

    barrier = pltpu.get_barrier_semaphore()

    @pl.loop(1, 16)
    def _(k):
        pl.semaphore_signal(
            barrier, inc=1, device_id=(s, lax.rem(b + k, NB), m), device_id_type=MESH
        )
        other = lax.rem(me + k, NG)
        pl.semaphore_signal(
            barrier, inc=1, device_id=(other // NM, b, lax.rem(other, NM)), device_id_type=MESH
        )

    l_ut.wait()
    l_mt.wait()
    f0 = 2 * m
    tile = jnp.concatenate(
        [
            tok_v[0, f0],
            tok_v[0, f0 + 1],
            tok_v[1, f0],
            tok_v[1, f0 + 1],
            jnp.zeros((8, 64), jnp.int32),
        ],
        axis=1,
    )
    tsend[...] = tile
    trecv[b] = tile
    pl.semaphore_wait(barrier, 30)
    tok = Spread("batch", lambda t, w: tsend, lambda w: trecv.at[b])
    tok.start()

    def up_send(block, **to):
        return send(upg.at[block], upg.at[block], **to)

    l_up.wait()
    u_y = up_send(me, ds=y1)
    u_p = up_send(me, dm=xp)
    u_m = up_send(me, dm=xm)
    wo_copies = []
    for yy in range(2):
        cols = pl.ds(pl.multiple_of((2 * yy + 1 - core) * 1024, 1024), 1024)
        wo_copies.append(send(wo_hbm.at[:, cols], wo_v.at[core, yy], ds=c1))

    lane = lax.broadcasted_iota(jnp.int32, (64, 128), 1)
    freq = jnp.exp(lax.rem(lane, 64).astype(F32) * (-2.0 * math.log(10000.0) / 128.0))
    frame = lax.rem(lax.broadcasted_iota(jnp.int32, (64, 128), 0), 8)

    @pl.loop(0, 8)
    def _(i):
        where = lax.broadcasted_iota(jnp.int32, (64, 128), 0) // 8
        pos = frame
        for d in range(8):
            pos = pos + jnp.where(where == d, len_ref[i * 8 + d], 0)
        angle = pos.astype(F32) * freq
        rows = pl.ds(pl.multiple_of(i * 64, 64), 64)
        cos_v[rows] = jnp.cos(angle)
        sine = jnp.sin(angle)
        sin_v[rows] = jnp.where(lane < 64, -sine, sine)

    l_g.wait()
    gain = g32_v[...].astype(F32)
    for i in range(32):
        g_v[:, pl.ds(128 * i, 128)] = gain[i : i + 1]

    u_y.wait_recv()
    yblk = y1 * NM + m
    u_yp = up_send(yblk, dm=xp)
    u_ym = up_send(yblk, dm=xm)

    tok.wait_recv()
    l_cb.wait()

    @pl.loop(0, NB)
    def _(i):
        tt[i] = trecv[i].T[:64]

    entry = lax.broadcasted_iota(jnp.int32, (32, 128), 1) + 128 * b
    pieces = Spread("batch", lambda t, w: part.at[w, t], lambda w: recv.at[w, b], 2)

    @pl.loop(0, 2)
    def _(which):
        @pl.loop(0, NB)
        def _(i):
            rows = tt[i, pl.ds(pl.multiple_of(32 * which, 32), 32), :]
            for c in range(8):
                hot = jnp.where(rows[:, c : c + 1] == entry, 1.0, 0.0).astype(BF16)
                oh[pl.ds(pl.multiple_of(i * 32, 32), 32), pl.ds(c * 128, 128)] = hot

        @pl.loop(0, 4)
        def _(i):
            rows = pl.ds(pl.multiple_of(i * 128, 128), 128)
            piece = dot(oh[rows], cb_v[...]).astype(BF16).reshape(4, 32, 256)
            part[which, pl.ds(4 * i, 4)] = piece

        pieces.start(which)
        recv[which, b] = part[which, b]

    u_p.wait_recv()
    u_f = up_send(s * NM + xm, dm=xp)
    u_m.wait_recv()
    u_yp.wait_recv()
    u_ym.wait_recv()
    u_yf = up_send(y1 * NM + xp, dm=xm)

    l_h.wait()
    l_w.wait()
    acc[...] = jnp.zeros_like(acc)

    @pl.loop(0, 8)
    def _(step):
        cols = pl.ds(pl.multiple_of(step * 512, 512), 512)
        scaled = (h_v[:, cols].astype(F32) * g_v[:, cols]).astype(BF16)
        for j in range(3):
            acc[j] += dot(scaled, w_v[j, cols, :])

    def total_of(which):
        def step(i, total):
            return total + recv[which, i].astype(F32)

        return lax.fori_loop(0, NB, step, jnp.zeros((32, 256), F32)).astype(BF16)

    pieces.wait_recv(0)
    lg[me] = total_of(0)
    latents = Spread("group", lambda t, w: lg.at[me], lambda w: lg.at[me])
    latents.start()

    u_f.wait_recv()
    u_yf.wait_recv()
    mine = pl.ds(pl.multiple_of(s * NM, NM), NM)
    yours = pl.ds(pl.multiple_of(y1 * NM, NM), NM)
    u_c = [up_send(mine, ds=c1), up_send(yours, ds=c1)]

    pieces.wait_recv(1)
    lmg[m] = total_of(1)
    lm_copies = [send(lmg.at[m], lmg.at[m], dm=t) for t in (xp, xm, xd)]

    mq[...] = jnp.zeros_like(mq)
    for copy in u_c:
        copy.wait_recv()

    @pl.loop(0, NG)
    def _(j):
        cols = pl.ds(pl.multiple_of(j * 256, 256), 256)
        scaled = (upg[j].astype(F32) * g_v[:, cols]).astype(BF16)
        for t in range(3):
            mq[t] += dot(scaled, w_v[t, cols, :])

    mqb[...] = mq[...].astype(BF16)

    latents.wait_recv()
    to = lax.broadcasted_iota(jnp.int32, (128, 128), 0)
    frm = lax.broadcasted_iota(jnp.int32, (128, 128), 1)
    perm = jnp.where(frm == lax.rem(to, 8) * 16 + to // 8, 1.0, 0.0).astype(BF16)

    @pl.loop(0, NS)
    def _(i):
        group = lg[pl.ds(NM * i, NM)].reshape(128, 256)
        lu[pl.ds(pl.multiple_of(128 * i, 128), 128)] = dot(perm, group).astype(BF16)

    ss[...] = jnp.zeros_like(ss)

    @pl.loop(0, NG)
    def _(j):
        cols = pl.ds(pl.multiple_of(j * 256, 256), 256)
        x0 = h_v[:, cols].astype(F32) + dot(lu[...], upg[j])
        sq = x0 * x0
        ss[...] += sq[:, :128] + sq[:, 128:]

    l_kv.wait()
    for copy in l_wo:
        copy.wait()
    for copy in wo_copies:
        copy.wait_recv()
    l_dp.wait()
    l_cw.wait()
    l_cs.wait()

    my_cols = pl.ds(pl.multiple_of(me * 256, 256), 256)
    row8 = lax.broadcasted_iota(jnp.int32, (32, 32), 0)
    col8 = lax.broadcasted_iota(jnp.int32, (32, 32), 1)
    new_ok = (row8 // 8 == col8 // 8) & (lax.rem(col8, 8) <= lax.rem(row8, 8))
    slot = lax.broadcasted_iota(jnp.int32, (8, 256), 1)

    def span(c, lower=0, count=CROWS):
        start = pl.multiple_of(c * CROWS + lower, CROWS // 2)
        return pl.ds(start, count)

    half = CROWS // 2

    def lo(c):
        return span(c, 0, half)

    def hi(c):
        return span(c, half, half)

    def attention(c):
        rows = span(c)
        r = lax.rsqrt(jnp.sum(ss[rows], axis=-1, keepdims=True) * (1.0 / WIDTH) + 1e-05)
        lat = lu[rows]
        q, k, v = [(acc[t, rows] + dot(lat, mqb[t])) * r for t in range(3)]
        cosine, sine = cos_v[rows], sin_v[rows]

        def rope(z):
            return (z * cosine + pltpu.roll(z, 64, 1) * sine).astype(BF16)

        for hd in range(2):
            cut = slice(128 * hd, 128 * hd + 128)
            qh, kh, vh = rope(q[:, cut]), rope(k[:, cut]), v[:, cut].astype(BF16)
            pieces = []
            for i in range(CROWS // 32):
                d0 = c * (CROWS // 8) + 4 * i
                sub = slice(32 * i, 32 * i + 32)
                keys = kv_v[0, pl.ds(d0, 4), hd].reshape(256, 128)
                values = kv_v[1, pl.ds(d0, 4), hd].reshape(256, 128)
                old = dot_t(qh[sub], keys) * (1.0 / math.sqrt(128.0))
                parts = []
                for d in range(4):
                    ok = (slot >= 64 * d) & (slot < 64 * d + len_ref[d0 + d])
                    parts.append(jnp.where(ok, old[8 * d : 8 * d + 8], NEG))
                old = jnp.concatenate(parts, axis=0)
                new = dot_t(qh[sub], kh[sub]) * (1.0 / math.sqrt(128.0))
                new = jnp.where(new_ok, new, NEG)
                top = jnp.maximum(
                    jnp.max(old, axis=-1, keepdims=True), jnp.max(new, axis=-1, keepdims=True)
                )
                old = jnp.exp(old - top)
                new = jnp.exp(new - top)
                total = jnp.sum(old, axis=-1, keepdims=True) + jnp.sum(
                    new, axis=-1, keepdims=True
                )
                mixed = dot(old.astype(BF16), values) + dot(new.astype(BF16), vh[sub])
                pieces.append((mixed / total).astype(BF16))
            attn_g[core, rows, pl.ds(128 * hd, 128)] = jnp.concatenate(pieces, axis=0)

    e_t = Event(lambda c: attn_g.at[core, span(c)], lambda c: attn_g.at[core, span(c)], ds=c1)
    lane_a, lane_b = pl.ds(0, 128), pl.ds(128, 128)
    e_ay = Event(lambda c: psend.at[1 - y, :, span(c), lane_a], lambda c: ra_y.at[:, span(c)], ds=y1)
    e_bp = Event(lambda c: psend.at[:, xd, lo(c), lane_b], lambda c: rbp.at[:, lo(c)], dm=xp)
    e_bm = Event(lambda c: psend.at[:, xd, hi(c), lane_b], lambda c: rbm.at[:, hi(c)], dm=xm)
    e_ap = Event(lambda c: a2.at[xd, lo(c)], lambda c: rap.at[lo(c)], dm=xp)
    e_am = Event(lambda c: a2.at[xd, hi(c)], lambda c: ram.at[hi(c)], dm=xm)
    e_bp2 = Event(lambda c: b2p.at[:, span(c)], lambda c: rb2p.at[:, span(c)], dm=xp)
    e_bm2 = Event(lambda c: b2m.at[:, span(c)], lambda c: rb2m.at[:, span(c)], dm=xm)
    e_ap2 = Event(lambda c: a3p.at[span(c)], lambda c: ra2p.at[span(c)], dm=xp)
    e_am2 = Event(lambda c: a3m.at[span(c)], lambda c: ra2m.at[span(c)], dm=xm)
    e_by = Event(lambda c: b_y.at[span(c)], lambda c: rby.at[span(c)], ds=y1)

    def gather(owner_s, owner_m, lane_half, rows, **to):
        def at(c):
            start = (owner_s * NM + owner_m) * 256 + 128 * lane_half
            return outv.at[rows(c), pl.ds(pl.multiple_of(start, 128), 128)]

        return Event(at, at, **to)

    g_a1 = gather(s, m, 0, span, ds=y1)
    g_a2 = gather(s, m, 0, span, dm=xp)
    g_a3 = gather(s, m, 0, span, dm=xm)
    g_a4 = gather(y1, m, 0, span, dm=xp)
    g_a5 = gather(y1, m, 0, span, dm=xm)
    g_a6 = gather(s, xm, 0, span, dm=xp)
    g_a7 = gather(y1, xp, 0, span, dm=xm)
    g_b1 = gather(s, m, 1, span, dm=xp)
    g_b2 = gather(s, m, 1, span, dm=xm)
    g_b3 = gather(s, m, 1, span, ds=y1)
    g_b4 = gather(s, xm, 1, lo, dm=xp)
    g_b5 = gather(s, xp, 1, hi, dm=xm)
    g_b6 = gather(s, xm, 1, span, ds=y1)
    g_b7 = gather(s, xp, 1, span, ds=y1)
    g_b8 = gather(s, xd, 1, lo, ds=y1)
    g_b9 = gather(s, xd, 1, hi, ds=y1)

    def wide(owner):
        def at(c):
            return outv.at[span(c), pl.ds(pl.multiple_of(owner * 1024, 1024), 1024)]

        return Event(at, at, ds=c1)

    g_f1 = wide(s)
    g_f2 = wide(y1)

    def stage_a(c):
        attention(c)
        e_t.start(c)

    def stage_o(c):
        e_t.wait(c)
        rows = span(c)
        for yy in range(2):
            proj = dot(attn_g[0, rows], wo_v[0, yy]) + dot(attn_g[1, rows], wo_v[1, yy])
            for t in range(NM):
                psend[yy, t, rows] = proj[:, 256 * t : 256 * t + 256].astype(BF16)
        e_ay.start(c)
        e_bp.start(c)
        e_bm.start(c)

    def stage_p(c):
        rows = span(c)
        e_bp.wait(c)
        e_bm.wait(c)
        for yy in range(2):
            b2p[yy, lo(c)] = (
                psend[yy, xp, lo(c), lane_b].astype(F32) + rbp[yy, lo(c)].astype(F32)
            ).astype(BF16)
            b2p[yy, hi(c)] = psend[yy, xp, hi(c), lane_b]
            b2m[yy, hi(c)] = (
                psend[yy, xm, hi(c), lane_b].astype(F32) + rbm[yy, hi(c)].astype(F32)
            ).astype(BF16)
            b2m[yy, lo(c)] = psend[yy, xm, lo(c), lane_b]
        e_bp2.start(c)
        e_bm2.start(c)
        e_ay.wait(c)
        for t in range(NM):
            a2[t, rows] = (
                psend[y, t, rows, lane_a].astype(F32) + ra_y[t, rows].astype(F32)
            ).astype(BF16)
        e_ap.start(c)
        e_am.start(c)

    def stage_q(c):
        rows = span(c)
        e_ap.wait(c)
        e_am.wait(c)
        a3p[lo(c)] = (a2[xp, lo(c)].astype(F32) + rap[lo(c)].astype(F32)).astype(BF16)
        a3p[hi(c)] = a2[xp, hi(c)]
        a3m[hi(c)] = (a2[xm, hi(c)].astype(F32) + ram[hi(c)].astype(F32)).astype(BF16)
        a3m[lo(c)] = a2[xm, lo(c)]
        e_ap2.start(c)
        e_am2.start(c)
        e_bp2.wait(c)
        e_bm2.wait(c)
        for where, yy in ((b_own, y), (b_y, 1 - y)):
            where[rows] = (
                psend[yy, m, rows, lane_b].astype(F32)
                + rb2p[yy, rows].astype(F32)
                + rb2m[yy, rows].astype(F32)
            ).astype(BF16)
        e_by.start(c)

    def stage_r(c):
        rows = span(c)
        x0 = h_v[rows, my_cols].astype(F32) + dot(lu[rows], upg[me])
        e_ap2.wait(c)
        e_am2.wait(c)
        first = a2[m, rows].astype(F32) + ra2p[rows].astype(F32) + ra2m[rows].astype(F32)
        e_by.wait(c)
        second = b_own[rows].astype(F32) + rby[rows].astype(F32)
        total = jnp.concatenate([first, second], axis=1)
        outv[rows, my_cols] = (x0 + total).astype(BF16)
        for event in (g_a1, g_b1, g_b2, g_a2, g_a3, g_b3):
            event.start(c)

    def stage_g(c):
        g_a1.wait(c)
        g_a4.start(c)
        g_a5.start(c)
        g_b1.wait(c)
        g_b4.start(c)
        g_b6.start(c)
        g_b2.wait(c)
        g_b5.start(c)
        g_b7.start(c)
        g_a2.wait(c)
        g_a6.start(c)

    def stage_h(c):
        g_a5.wait(c)
        g_a7.start(c)
        g_b4.wait(c)
        g_b8.start(c)
        g_b5.wait(c)
        g_b9.start(c)

    def stage_i(c):
        for event in (g_a3, g_a4, g_a6, g_a7, g_b3, g_b6, g_b7, g_b8, g_b9):
            event.wait(c)
        g_f1.start(c)
        g_f2.start(c)

    def stage_j(c):
        g_f1.wait(c)
        g_f2.wait(c)

    def excite(layer, state):
        excited = jnp.where(state > 0, state, jnp.exp(jnp.minimum(state, 0.0)) - 1.0)
        place = el_v.at[layer, pl.ds(32, 128), pl.ds(pl.multiple_of(m * 128, 128), 128)]
        place[...] = excited.astype(BF16)
        st_v[...] = state

    def codec_at(layer):
        return el_v.at[layer, pl.ds(32, 128), pl.ds(pl.multiple_of(m * 128, 128), 128)]

    codec_moves = [Event(codec_at, codec_at, dm=t) for t in (xp, xm, xd)]

    def codec_start():
        for copy in lm_copies:
            copy.wait_recv()
        excite(0, dot(lmg[...].reshape(128, 256), dp_v[...]))
        for move in codec_moves:
            move.start(0)

        @pl.loop(0, 4)
        def _(layer):
            rows = [cs_v[d, layer].astype(F32) for d in range(16)]
            for j in range(2):
                el_v[layer, pl.ds(16 * j, 16), :] = jnp.concatenate(
                    [row[j : j + 1] for row in rows], axis=0
                ).astype(BF16)

    def codec_step(layer):
        for move in codec_moves:
            move.wait(layer)
        state = st_v[...]
        for tap in range(3):
            state = state + dot(el_v[layer, pl.ds(16 * tap, 128), :], cw_v[layer, tap])
        st_v[...] = state

        @pl.when(layer < 3)
        def _():
            excite(layer + 1, state)
            for move in codec_moves:
                move.start(layer + 1)

    stages = [stage_j, stage_i, stage_h, stage_g, stage_r, stage_q, stage_p, stage_o]

    codec_start()

    @pl.loop(0, NCHUNK + len(stages))
    def _(step):
        pl.when(step < NCHUNK)(lambda: stage_a(step))
        for place, stage in enumerate(stages):
            c = step - (len(stages) - place)

            @pl.when((c >= 0) & (c < NCHUNK))
            def _():
                stage(c)

        @pl.when((step >= 1) & (step < 5))
        def _():
            codec_step(step - 1)

    decv[...] = dot(perm, st_v[...].astype(BF16)).astype(BF16)
    for done in finish:
        done()


N_LOCAL = 16
N_REMOTE = 256


def per_device(
    hidden_in,
    model_tokens,
    user_tokens,
    codebooks,
    decode_proj,
    conv_weight,
    conv_state,
    user_proj,
    norm_gain,
    w_qkv,
    w_out,
    kv_cache,
    cache_len,
):
    any_space = pl.BlockSpec(memory_space=pl.ANY)
    smem = pl.BlockSpec(memory_space=pltpu.SMEM)
    vmem = pltpu.VMEM
    out, dec = pl.pallas_call(
        kernel,
        out_shape=(vmem((ROWS, WIDTH), BF16), vmem((128, 128), BF16)),
        in_specs=[any_space] * 12 + [smem],
        out_specs=(pl.BlockSpec(memory_space=vmem), pl.BlockSpec(memory_space=vmem)),
        scratch_shapes=[
            vmem((ROWS, WIDTH), BF16),
            vmem((2, 8, 8, 16), jnp.int32),
            vmem((1024, 256), BF16),
            vmem((256, 128), BF16),
            vmem((4, 3, 512, 128), BF16),
            vmem((16, 4, 2, 512), BF16),
            vmem((4, 160, 512), BF16),
            vmem((128, 128), F32),
            vmem((32, 128), BF16),
            vmem((1, WIDTH), F32),
            vmem((3, WIDTH, 256), BF16),
            vmem((2, 2, 256, 1024), BF16),
            vmem((2, 64, 2, 64, 128), BF16),
            vmem((NG, 256, 256), BF16),
            vmem((8, 128), jnp.int32),
            vmem((NB, 8, 128), jnp.int32),
            vmem((NB, 64, 8), jnp.int32),
            vmem((512, 1024), BF16),
            vmem((2, NB, 32, 256), BF16),
            vmem((2, NB, 32, 256), BF16),
            vmem((NG, 32, 256), BF16),
            vmem((NM, 32, 256), BF16),
            vmem((ROWS, 256), BF16),
            vmem((3, 256, 256), F32),
            vmem((3, 256, 256), BF16),
            vmem((3, ROWS, 256), F32),
            vmem((ROWS, 128), F32),
            vmem((ROWS, 128), F32),
            vmem((ROWS, 128), F32),
            vmem((2, ROWS, 256), BF16),
            vmem((2, NM, ROWS, 256), BF16),
            vmem((NM, ROWS, 128), BF16),
            vmem((NM, ROWS, 128), BF16),
            vmem((ROWS, 128), BF16),
            vmem((ROWS, 128), BF16),
            vmem((ROWS, 128), BF16),
            vmem((ROWS, 128), BF16),
            vmem((ROWS, 128), BF16),
            vmem((ROWS, 128), BF16),
            vmem((2, ROWS, 128), BF16),
            vmem((2, ROWS, 128), BF16),
            vmem((2, ROWS, 128), BF16),
            vmem((2, ROWS, 128), BF16),
            vmem((2, ROWS, 128), BF16),
            vmem((2, ROWS, 128), BF16),
            vmem((ROWS, 128), BF16),
            vmem((ROWS, 128), BF16),
            vmem((ROWS, 128), BF16),
            pltpu.SemaphoreType.DMA((N_LOCAL,)),
            pltpu.SemaphoreType.DMA((N_REMOTE,)),
            pltpu.SemaphoreType.DMA((N_REMOTE,)),
        ],
        compiler_params=pltpu.CompilerParams(
            collective_id=0, has_side_effects=True, vmem_limit_bytes=59 * 1024 * 1024
        ),
        cost_estimate=pl.CostEstimate(
            flops=12_000_000_000, bytes_accessed=30_000_000, transcendentals=1_000_000
        ),
    )(
        hidden_in.reshape(ROWS, WIDTH),
        jnp.transpose(model_tokens, (1, 2, 0)),
        jnp.transpose(user_tokens, (1, 2, 0)),
        codebooks.reshape(1024, 256),
        decode_proj,
        conv_weight,
        conv_state,
        user_proj,
        norm_gain.reshape(32, 128),
        jnp.transpose(w_qkv, (1, 0, 2)),
        w_out,
        kv_cache,
        cache_len,
    )
    return out.reshape(64, 8, WIDTH), dec.reshape(16, 8, 128)


def solution(mesh):
    in_specs = (
        P("batch", None, None),
        P(("batch", "section"), None, None),
        P(("batch", "section"), None, None),
        P(None, "batch", None),
        P(None, "mp"),
        P(None, None, None, "mp"),
        P(("batch", "section"), None, None, None),
        P(None, ("section", "mp")),
        P(),
        P(None, None, ("section", "mp")),
        P(("section", "mp"), None),
        P(None, "batch", ("section", "mp"), None, None),
        P("batch"),
    )
    out_specs = (P("batch", None, None), P(("batch", "section"), None, "mp"))
    return jax.shard_map(
        per_device, mesh=mesh, in_specs=in_specs, out_specs=out_specs, check_vma=False
    )
```

time: 118 us -> 102 us (0.86)
  Pallas kernels: 108 us -> 98.9 us
  local copies, waits for them, and re-layouts: 6.92 us -> 2.63 us
  other arithmetic: 1.3 us -> 0 us
    pallas_call x1, Pallas kernels: 108 us -> 98.9 us  [per_device(): pl.pallas_call(kernel, out_shape=(vmem((ROWS, WIDTH), BF16), vmem((128, 1...]
    unnamed x4 -> x2, local copies, waits for them, and re-layouts: 5.32 us -> 2.63 us
    transpose x1 -> x0, local copies, waits for them, and re-layouts: 1.6 us -> none  [per_device(): jnp.transpose(conv_state, (1, 2, 0, 3)).reshape(4, 32, 512)]
    reshape x1 -> x0, other arithmetic: 1.3 us -> none  [per_device(): norm_gain.astype(F32).reshape(1, WIDTH)]
where the time goes in v2:
time: 102 us
  Pallas kernels  98.9 us (97%)
  local copies, waits for them, and re-layouts  2.63 us (3%)
    pallas_call x1, Pallas kernels, per_device(): pl.pallas_call(kernel, out_shape=(vmem((ROWS, WIDTH), BF16), vmem((128, 1...  98.9 us
    unnamed x2, local copies, waits for them, and re-layouts  2.63 us

profile of v2, /device:TPU:1, one launch (start us, length us, event | category | flops | bytes accessed | tf_op | source)
XLA Modules:
  0.0 102.2 jit_solution(6337756674586399191)
XLA Ops:
  0.6 98.9 %shard_map.140 = (bf16[512,4096]{1,0:T(8,128)(2,1)S(1)}, bf16[128,128]{1,0:T(8,128)(2,1)S(1)}) custom-call(bf16[512,4096]{1,0:T(8,128)(2,1)} %bitcast.11, s32[8,8,16]{2,1,0:T(8,128)} %bitcast.13, s32[8,8,16]{2,1,0:T(8,128)} %bitcast.14, bf16[1024,256]{1,0:T(8,128)(2,1)} %bitcast.12, bf16[256,128]{1,0:T(8,128)(2,1)} %dp_hbm.1, ...), custom_call_target="tpu_custom_call" | custom-call | flops 12000000000 | bytes 30000000 | tf_op jit(solution)/shard_map/pallas_call | solution.py:691
  99.5 2.0 %copy.17 = bf16[64,8,4096]{2,1,0:T(8,128)(2,1)} copy(bf16[64,8,4096]{2,1,0:T(8,128)(2,1)S(1)} %bitcast.8) | data formatting | bytes 8388608
  101.5 0.6 copy.18

commit v3 on v2

--- a/solution.py
+++ b/solution.py
@@ -72,7 +72,6 @@
     tsend,
     trecv,
     tt,
-    oh,
     part,
     recv,
     lg,
@@ -90,14 +89,10 @@
     a2,
     rap,
     ram,
-    a3p,
-    a3m,
     ra2p,
     ra2m,
     rbp,
     rbm,
-    b2p,
-    b2m,
     rb2p,
     rb2m,
     b_own,
@@ -158,10 +153,10 @@
             at = self.base + 15 * which + k - 1
             if self.axis == "batch":
                 target = lax.rem(b + k, NB)
-                return remote_copy(self.src(target, which), self.dst(which), at, db=target)
+                return remote_copy(self.src(k, which), self.dst(which), at, db=target)
             target = lax.rem(me + k, NG)
             return remote_copy(
-                self.src(target, which),
+                self.src(k, which),
                 self.dst(which),
                 at,
                 ds=target // NM,
@@ -204,6 +199,18 @@
             @pl.loop(0, self.count)
             def _(c):
                 self.make(c).wait_send()
+
+    barrier = pltpu.get_barrier_semaphore()
+
+    @pl.loop(1, 16)
+    def _(k):
+        pl.semaphore_signal(
+            barrier, inc=1, device_id=(s, lax.rem(b + k, NB), m), device_id_type=MESH
+        )
+        other = lax.rem(me + k, NG)
+        pl.semaphore_signal(
+            barrier, inc=1, device_id=(other // NM, b, lax.rem(other, NM)), device_id_type=MESH
+        )
 
     l_ut = load(ut_hbm, tok_v.at[0])
     l_mt = load(mt_hbm, tok_v.at[1])
@@ -220,18 +227,6 @@
     l_kv = load(kv_hbm, kv_v)
     l_dp = load(dp_hbm, dp_v)
     l_cw = load(cw_hbm, cw_v)
-
-    barrier = pltpu.get_barrier_semaphore()
-
-    @pl.loop(1, 16)
-    def _(k):
-        pl.semaphore_signal(
-            barrier, inc=1, device_id=(s, lax.rem(b + k, NB), m), device_id_type=MESH
-        )
-        other = lax.rem(me + k, NG)
-        pl.semaphore_signal(
-            barrier, inc=1, device_id=(other // NM, b, lax.rem(other, NM)), device_id_type=MESH
-        )
 
     l_ut.wait()
     l_mt.wait()
@@ -249,7 +244,7 @@
     tsend[...] = tile
     trecv[b] = tile
     pl.semaphore_wait(barrier, 30)
-    tok = Spread("batch", lambda t, w: tsend, lambda w: trecv.at[b])
+    tok = Spread("batch", lambda k, w: tsend, lambda w: trecv.at[b])
     tok.start()
 
     def up_send(block, **to):
@@ -294,29 +289,33 @@
     l_cb.wait()
 
     @pl.loop(0, NB)
-    def _(i):
-        tt[i] = trecv[i].T[:64]
-
-    entry = lax.broadcasted_iota(jnp.int32, (32, 128), 1) + 128 * b
-    pieces = Spread("batch", lambda t, w: part.at[w, t], lambda w: recv.at[w, b], 2)
-
-    @pl.loop(0, 2)
-    def _(which):
-        @pl.loop(0, NB)
-        def _(i):
-            rows = tt[i, pl.ds(pl.multiple_of(32 * which, 32), 32), :]
-            for c in range(8):
-                hot = jnp.where(rows[:, c : c + 1] == entry, 1.0, 0.0).astype(BF16)
-                oh[pl.ds(pl.multiple_of(i * 32, 32), 32), pl.ds(c * 128, 128)] = hot
-
+    def _(k):
+        tt[k] = trecv[lax.rem(b + k, NB)].T[:64]
+
+    entry = lax.broadcasted_iota(jnp.int32, (128, 128), 1) + 128 * b
+    pieces = Spread("batch", lambda k, w: part.at[w, k], lambda w: recv.at[w, b], 2)
+
+    def look_up(which):
         @pl.loop(0, 4)
-        def _(i):
-            rows = pl.ds(pl.multiple_of(i * 128, 128), 128)
-            piece = dot(oh[rows], cb_v[...]).astype(BF16).reshape(4, 32, 256)
-            part[which, pl.ds(4 * i, 4)] = piece
-
-        pieces.start(which)
-        recv[which, b] = part[which, b]
+        def _(quad):
+            rows = tt[pl.ds(4 * quad, 4), pl.ds(32 * which, 32), :].reshape(128, 8)
+            hot = [jnp.where(rows[:, c : c + 1] == entry, 1.0, 0.0).astype(BF16) for c in range(8)]
+            piece = dot(jnp.concatenate(hot, axis=1), cb_v[...])
+            part[which, pl.ds(4 * quad, 4)] = piece.astype(BF16).reshape(4, 32, 256)
+
+            if which == 0:
+
+                @pl.loop(0, 4)
+                def _(j):
+                    k = 4 * quad + j
+
+                    @pl.when(k > 0)
+                    def _():
+                        pieces.make(k, which).start()
+
+        recv[which, b] = part[which, 0]
+
+    look_up(0)
 
     u_p.wait_recv()
     u_f = up_send(s * NM + xm, dm=xp)
@@ -325,27 +324,28 @@
     u_ym.wait_recv()
     u_yf = up_send(y1 * NM + xp, dm=xm)
 
+    l_cs.wait()
+
+    @pl.loop(0, 4)
+    def _(layer):
+        rows = [cs_v[d, layer].astype(F32) for d in range(16)]
+        for j in range(2):
+            el_v[layer, pl.ds(16 * j, 16), :] = jnp.concatenate(
+                [row[j : j + 1] for row in rows], axis=0
+            ).astype(BF16)
+
     l_h.wait()
     l_w.wait()
     acc[...] = jnp.zeros_like(acc)
 
-    @pl.loop(0, 8)
+    @pl.loop(0, 4)
     def _(step):
-        cols = pl.ds(pl.multiple_of(step * 512, 512), 512)
+        cols = pl.ds(pl.multiple_of(step * 1024, 1024), 1024)
         scaled = (h_v[:, cols].astype(F32) * g_v[:, cols]).astype(BF16)
         for j in range(3):
             acc[j] += dot(scaled, w_v[j, cols, :])
 
-    def total_of(which):
-        def step(i, total):
-            return total + recv[which, i].astype(F32)
-
-        return lax.fori_loop(0, NB, step, jnp.zeros((32, 256), F32)).astype(BF16)
-
-    pieces.wait_recv(0)
-    lg[me] = total_of(0)
-    latents = Spread("group", lambda t, w: lg.at[me], lambda w: lg.at[me])
-    latents.start()
+    look_up(1)
 
     u_f.wait_recv()
     u_yf.wait_recv()
@@ -353,18 +353,27 @@
     yours = pl.ds(pl.multiple_of(y1 * NM, NM), NM)
     u_c = [up_send(mine, ds=c1), up_send(yours, ds=c1)]
 
-    pieces.wait_recv(1)
-    lmg[m] = total_of(1)
-    lm_copies = [send(lmg.at[m], lmg.at[m], dm=t) for t in (xp, xm, xd)]
+    def total_of(which):
+        def step(i, total):
+            return total + recv[which, i].astype(F32)
+
+        return lax.fori_loop(0, NB, step, jnp.zeros((32, 256), F32)).astype(BF16)
+
+    pieces.wait_recv(0)
+    lg[me] = total_of(0)
+    latents = Spread("group", lambda k, w: lg.at[me], lambda w: lg.at[me])
+    latents.start()
+    pieces.start(1)
 
     mq[...] = jnp.zeros_like(mq)
     for copy in u_c:
         copy.wait_recv()
 
-    @pl.loop(0, NG)
+    @pl.loop(0, NS)
     def _(j):
-        cols = pl.ds(pl.multiple_of(j * 256, 256), 256)
-        scaled = (upg[j].astype(F32) * g_v[:, cols]).astype(BF16)
+        cols = pl.ds(pl.multiple_of(j * 1024, 1024), 1024)
+        wide_up = jnp.concatenate([upg[NM * j + i] for i in range(NM)], axis=1)
+        scaled = (wide_up.astype(F32) * g_v[:, cols]).astype(BF16)
         for t in range(3):
             mq[t] += dot(scaled, w_v[t, cols, :])
 
@@ -382,7 +391,7 @@
 
     ss[...] = jnp.zeros_like(ss)
 
-    @pl.loop(0, NG)
+    @pl.loop(0, NG, unroll=2)
     def _(j):
         cols = pl.ds(pl.multiple_of(j * 256, 256), 256)
         x0 = h_v[:, cols].astype(F32) + dot(lu[...], upg[j])
@@ -396,7 +405,6 @@
         copy.wait_recv()
     l_dp.wait()
     l_cw.wait()
-    l_cs.wait()
 
     my_cols = pl.ds(pl.multiple_of(me * 256, 256), 256)
     row8 = lax.broadcasted_iota(jnp.int32, (32, 32), 0)
@@ -462,44 +470,32 @@
     e_bm = Event(lambda c: psend.at[:, xd, hi(c), lane_b], lambda c: rbm.at[:, hi(c)], dm=xm)
     e_ap = Event(lambda c: a2.at[xd, lo(c)], lambda c: rap.at[lo(c)], dm=xp)
     e_am = Event(lambda c: a2.at[xd, hi(c)], lambda c: ram.at[hi(c)], dm=xm)
-    e_bp2 = Event(lambda c: b2p.at[:, span(c)], lambda c: rb2p.at[:, span(c)], dm=xp)
-    e_bm2 = Event(lambda c: b2m.at[:, span(c)], lambda c: rb2m.at[:, span(c)], dm=xm)
-    e_ap2 = Event(lambda c: a3p.at[span(c)], lambda c: ra2p.at[span(c)], dm=xp)
-    e_am2 = Event(lambda c: a3m.at[span(c)], lambda c: ra2m.at[span(c)], dm=xm)
+    e_bp2 = Event(lambda c: psend.at[:, xp, span(c), lane_b], lambda c: rb2p.at[:, span(c)], dm=xp)
+    e_bm2 = Event(lambda c: psend.at[:, xm, span(c), lane_b], lambda c: rb2m.at[:, span(c)], dm=xm)
+    e_ap2 = Event(lambda c: a2.at[xp, span(c)], lambda c: ra2p.at[span(c)], dm=xp)
+    e_am2 = Event(lambda c: a2.at[xm, span(c)], lambda c: ra2m.at[span(c)], dm=xm)
     e_by = Event(lambda c: b_y.at[span(c)], lambda c: rby.at[span(c)], ds=y1)
 
-    def gather(owner_s, owner_m, lane_half, rows, **to):
+    def gather(owner, first, count, **to):
         def at(c):
-            start = (owner_s * NM + owner_m) * 256 + 128 * lane_half
-            return outv.at[rows(c), pl.ds(pl.multiple_of(start, 128), 128)]
+            start = pl.multiple_of(owner * 256 + first, 128)
+            return outv.at[span(c), pl.ds(start, count)]
 
         return Event(at, at, **to)
 
-    g_a1 = gather(s, m, 0, span, ds=y1)
-    g_a2 = gather(s, m, 0, span, dm=xp)
-    g_a3 = gather(s, m, 0, span, dm=xm)
-    g_a4 = gather(y1, m, 0, span, dm=xp)
-    g_a5 = gather(y1, m, 0, span, dm=xm)
-    g_a6 = gather(s, xm, 0, span, dm=xp)
-    g_a7 = gather(y1, xp, 0, span, dm=xm)
-    g_b1 = gather(s, m, 1, span, dm=xp)
-    g_b2 = gather(s, m, 1, span, dm=xm)
-    g_b3 = gather(s, m, 1, span, ds=y1)
-    g_b4 = gather(s, xm, 1, lo, dm=xp)
-    g_b5 = gather(s, xp, 1, hi, dm=xm)
-    g_b6 = gather(s, xm, 1, span, ds=y1)
-    g_b7 = gather(s, xp, 1, span, ds=y1)
-    g_b8 = gather(s, xd, 1, lo, ds=y1)
-    g_b9 = gather(s, xd, 1, hi, ds=y1)
-
-    def wide(owner):
-        def at(c):
-            return outv.at[span(c), pl.ds(pl.multiple_of(owner * 1024, 1024), 1024)]
-
-        return Event(at, at, ds=c1)
-
-    g_f1 = wide(s)
-    g_f2 = wide(y1)
+    g_p = gather(me, 0, 256, dm=xp)
+    g_m = gather(me, 0, 256, dm=xm)
+    g_y = gather(me, 0, 256, ds=y1)
+    g_ap = gather(y1 * NM + m, 0, 128, dm=xp)
+    g_am = gather(y1 * NM + m, 0, 128, dm=xm)
+    g_pp = gather(s * NM + xm, 0, 128, dm=xp)
+    g_mm = gather(s * NM + xp, 128, 128, dm=xm)
+    g_bm = gather(s * NM + xm, 128, 128, ds=y1)
+    g_bp = gather(s * NM + xp, 128, 128, ds=y1)
+    g_ad = gather(y1 * NM + xm, 0, 128, dm=xp)
+    g_bd = gather(s * NM + xd, 128, 128, ds=y1)
+    g_f1 = gather(s * NM, 0, 1024, ds=c1)
+    g_f2 = gather(y1 * NM, 0, 1024, ds=c1)
 
     def stage_a(c):
         attention(c)
@@ -516,48 +512,42 @@
         e_bp.start(c)
         e_bm.start(c)
 
+    def add(place, other):
+        place[...] = (place[...].astype(F32) + other.astype(F32)).astype(BF16)
+
     def stage_p(c):
         rows = span(c)
         e_bp.wait(c)
+        add(psend.at[:, xp, lo(c), lane_b], rbp[:, lo(c)])
+        e_bp2.start(c)
         e_bm.wait(c)
-        for yy in range(2):
-            b2p[yy, lo(c)] = (
-                psend[yy, xp, lo(c), lane_b].astype(F32) + rbp[yy, lo(c)].astype(F32)
-            ).astype(BF16)
-            b2p[yy, hi(c)] = psend[yy, xp, hi(c), lane_b]
-            b2m[yy, hi(c)] = (
-                psend[yy, xm, hi(c), lane_b].astype(F32) + rbm[yy, hi(c)].astype(F32)
-            ).astype(BF16)
-            b2m[yy, lo(c)] = psend[yy, xm, lo(c), lane_b]
-        e_bp2.start(c)
+        add(psend.at[:, xm, hi(c), lane_b], rbm[:, hi(c)])
         e_bm2.start(c)
         e_ay.wait(c)
-        for t in range(NM):
-            a2[t, rows] = (
-                psend[y, t, rows, lane_a].astype(F32) + ra_y[t, rows].astype(F32)
-            ).astype(BF16)
+        a2[:, rows] = (
+            psend[y, :, rows, lane_a].astype(F32) + ra_y[:, rows].astype(F32)
+        ).astype(BF16)
         e_ap.start(c)
         e_am.start(c)
 
     def stage_q(c):
         rows = span(c)
         e_ap.wait(c)
+        add(a2.at[xp, lo(c)], rap[lo(c)])
+        e_ap2.start(c)
         e_am.wait(c)
-        a3p[lo(c)] = (a2[xp, lo(c)].astype(F32) + rap[lo(c)].astype(F32)).astype(BF16)
-        a3p[hi(c)] = a2[xp, hi(c)]
-        a3m[hi(c)] = (a2[xm, hi(c)].astype(F32) + ram[hi(c)].astype(F32)).astype(BF16)
-        a3m[lo(c)] = a2[xm, lo(c)]
-        e_ap2.start(c)
+        add(a2.at[xm, hi(c)], ram[hi(c)])
         e_am2.start(c)
         e_bp2.wait(c)
         e_bm2.wait(c)
-        for where, yy in ((b_own, y), (b_y, 1 - y)):
-            where[rows] = (
-                psend[yy, m, rows, lane_b].astype(F32)
-                + rb2p[yy, rows].astype(F32)
-                + rb2m[yy, rows].astype(F32)
-            ).astype(BF16)
+
+        def total(yy):
+            ours = psend[yy, m, rows, lane_b].astype(F32)
+            return ours + rb2p[yy, rows].astype(F32) + rb2m[yy, rows].astype(F32)
+
+        b_y[rows] = total(1 - y).astype(BF16)
         e_by.start(c)
+        b_own[rows] = total(y)
 
     def stage_r(c):
         rows = span(c)
@@ -566,37 +556,34 @@
         e_am2.wait(c)
         first = a2[m, rows].astype(F32) + ra2p[rows].astype(F32) + ra2m[rows].astype(F32)
         e_by.wait(c)
-        second = b_own[rows].astype(F32) + rby[rows].astype(F32)
+        second = b_own[rows] + rby[rows].astype(F32)
         total = jnp.concatenate([first, second], axis=1)
         outv[rows, my_cols] = (x0 + total).astype(BF16)
-        for event in (g_a1, g_b1, g_b2, g_a2, g_a3, g_b3):
+        for event in (g_y, g_p, g_m):
             event.start(c)
 
     def stage_g(c):
-        g_a1.wait(c)
-        g_a4.start(c)
-        g_a5.start(c)
-        g_b1.wait(c)
-        g_b4.start(c)
-        g_b6.start(c)
-        g_b2.wait(c)
-        g_b5.start(c)
-        g_b7.start(c)
-        g_a2.wait(c)
-        g_a6.start(c)
+        g_y.wait(c)
+        g_ap.start(c)
+        g_am.start(c)
+        g_p.wait(c)
+        g_pp.start(c)
+        g_bm.start(c)
+        g_m.wait(c)
+        g_mm.start(c)
+        g_bp.start(c)
 
     def stage_h(c):
-        g_a5.wait(c)
-        g_a7.start(c)
-        g_b4.wait(c)
-        g_b8.start(c)
-        g_b5.wait(c)
-        g_b9.start(c)
+        g_ap.wait(c)
+        g_ad.start(c)
+        g_mm.wait(c)
+        g_bd.start(c)
+        g_pp.wait(c)
+        g_f1.start(c)
 
     def stage_i(c):
-        for event in (g_a3, g_a4, g_a6, g_a7, g_b3, g_b6, g_b7, g_b8, g_b9):
+        for event in (g_am, g_bm, g_bp, g_ad, g_bd):
             event.wait(c)
-        g_f1.start(c)
         g_f2.start(c)
 
     def stage_j(c):
@@ -612,22 +599,22 @@
     def codec_at(layer):
         return el_v.at[layer, pl.ds(32, 128), pl.ds(pl.multiple_of(m * 128, 128), 128)]
 
-    codec_moves = [Event(codec_at, codec_at, dm=t) for t in (xp, xm, xd)]
+    codec_moves = [Event(codec_at, codec_at, 4, dm=t) for t in (xp, xm, xd)]
+
+    lm_moves = [Event(lambda c: lmg.at[m], lambda c: lmg.at[m], 1, dm=t) for t in (xp, xm, xd)]
+
+    def codec_latents():
+        pieces.wait_recv(1)
+        lmg[m] = total_of(1)
+        for move in lm_moves:
+            move.start(0)
 
     def codec_start():
-        for copy in lm_copies:
-            copy.wait_recv()
+        for move in lm_moves:
+            move.wait(0)
         excite(0, dot(lmg[...].reshape(128, 256), dp_v[...]))
         for move in codec_moves:
             move.start(0)
-
-        @pl.loop(0, 4)
-        def _(layer):
-            rows = [cs_v[d, layer].astype(F32) for d in range(16)]
-            for j in range(2):
-                el_v[layer, pl.ds(16 * j, 16), :] = jnp.concatenate(
-                    [row[j : j + 1] for row in rows], axis=0
-                ).astype(BF16)
 
     def codec_step(layer):
         for move in codec_moves:
@@ -645,8 +632,6 @@
 
     stages = [stage_j, stage_i, stage_h, stage_g, stage_r, stage_q, stage_p, stage_o]
 
-    codec_start()
-
     @pl.loop(0, NCHUNK + len(stages))
     def _(step):
         pl.when(step < NCHUNK)(lambda: stage_a(step))
@@ -657,9 +642,12 @@
             def _():
                 stage(c)
 
-        @pl.when((step >= 1) & (step < 5))
+        pl.when(step == 2)(codec_latents)
+        pl.when(step == 3)(codec_start)
+
+        @pl.when((step >= 4) & (step < 8))
         def _():
-            codec_step(step - 1)
+            codec_step(step - 4)
 
     decv[...] = dot(perm, st_v[...].astype(BF16)).astype(BF16)
     for done in finish:
@@ -711,7 +699,6 @@
             vmem((8, 128), jnp.int32),
             vmem((NB, 8, 128), jnp.int32),
             vmem((NB, 64, 8), jnp.int32),
-            vmem((512, 1024), BF16),
             vmem((2, NB, 32, 256), BF16),
             vmem((2, NB, 32, 256), BF16),
             vmem((NG, 32, 256), BF16),
@@ -731,15 +718,11 @@
             vmem((ROWS, 128), BF16),
             vmem((ROWS, 128), BF16),
             vmem((ROWS, 128), BF16),
-            vmem((ROWS, 128), BF16),
-            vmem((ROWS, 128), BF16),
             vmem((2, ROWS, 128), BF16),
             vmem((2, ROWS, 128), BF16),
             vmem((2, ROWS, 128), BF16),
             vmem((2, ROWS, 128), BF16),
-            vmem((2, ROWS, 128), BF16),
-            vmem((2, ROWS, 128), BF16),
-            vmem((ROWS, 128), BF16),
+            vmem((ROWS, 128), F32),
             vmem((ROWS, 128), BF16),
             vmem((ROWS, 128), BF16),
             pltpu.SemaphoreType.DMA((N_LOCAL,)),

time: 102 us -> 96.7 us (0.948)
  Pallas kernels: 98.9 us -> 93.4 us
    pallas_call x1, Pallas kernels: 98.9 us -> 93.4 us  [per_device(): pl.pallas_call(kernel, out_shape=(vmem((ROWS, WIDTH), BF16), vmem((128, 1...]
where the time goes in v3:
time: 96.7 us; the launch traced here: 96.6 us
  Pallas kernels  93.4 us (97%)
  local copies, waits for them, and re-layouts  2.63 us (3%)
    pallas_call x1, Pallas kernels, per_device(): pl.pallas_call(kernel, out_shape=(vmem((ROWS, WIDTH), BF16), vmem((128, 1...  93.4 us
    unnamed x2, local copies, waits for them, and re-layouts  2.63 us

profile of v3, /device:TPU:1, one launch (start us, length us, event | category | flops | bytes accessed | tf_op | source)
XLA Modules:
  0.0 96.6 jit_solution(3870116022030847473)
XLA Ops:
  0.6 93.4 %shard_map.140 = (bf16[512,4096]{1,0:T(8,128)(2,1)S(1)}, bf16[128,128]{1,0:T(8,128)(2,1)S(1)}) custom-call(bf16[512,4096]{1,0:T(8,128)(2,1)} %bitcast.11, s32[8,8,16]{2,1,0:T(8,128)} %bitcast.13, s32[8,8,16]{2,1,0:T(8,128)} %bitcast.14, bf16[1024,256]{1,0:T(8,128)(2,1)} %bitcast.12, bf16[256,128]{1,0:T(8,128)(2,1)} %dp_hbm.1, ...), custom_call_target="tpu_custom_call" | custom-call | flops 12000000000 | bytes 30000000 | tf_op jit(solution)/shard_map/pallas_call | solution.py:679
  94.0 2.0 %copy.17 = bf16[64,8,4096]{2,1,0:T(8,128)(2,1)} copy(bf16[64,8,4096]{2,1,0:T(8,128)(2,1)S(1)} %bitcast.8) | data formatting | bytes 8388608
  96.0 0.6 copy.18

commit v4 on v3

--- a/solution.py
+++ b/solution.py
@@ -630,24 +630,24 @@
             for move in codec_moves:
                 move.start(layer + 1)
 
-    stages = [stage_j, stage_i, stage_h, stage_g, stage_r, stage_q, stage_p, stage_o]
+    stages = [stage_o, stage_p, stage_q, stage_r, stage_g, stage_h, stage_i, stage_j]
 
     @pl.loop(0, NCHUNK + len(stages))
     def _(step):
         pl.when(step < NCHUNK)(lambda: stage_a(step))
         for place, stage in enumerate(stages):
-            c = step - (len(stages) - place)
+            c = step - 1 - place
 
             @pl.when((c >= 0) & (c < NCHUNK))
             def _():
                 stage(c)
 
-        pl.when(step == 2)(codec_latents)
-        pl.when(step == 3)(codec_start)
-
-        @pl.when((step >= 4) & (step < 8))
+        pl.when(step == 1)(codec_latents)
+        pl.when(step == 2)(codec_start)
+
+        @pl.when((step >= 3) & (step < 7))
         def _():
-            codec_step(step - 4)
+            codec_step(step - 3)
 
     decv[...] = dot(perm, st_v[...].astype(BF16)).astype(BF16)
     for done in finish:

time: 96.7 us -> 93.6 us (0.968)
  Pallas kernels: 93.4 us -> 90.3 us
    pallas_call x1, Pallas kernels: 93.4 us -> 90.3 us  [per_device(): pl.pallas_call(kernel, out_shape=(vmem((ROWS, WIDTH), BF16), vmem((128, 1...]
where the time goes in v4:
time: 93.6 us; the launch traced here: 93.5 us
  Pallas kernels  90.3 us (96%)
  local copies, waits for them, and re-layouts  2.63 us (3%)
    pallas_call x1, Pallas kernels, per_device(): pl.pallas_call(kernel, out_shape=(vmem((ROWS, WIDTH), BF16), vmem((128, 1...  90.3 us
    unnamed x2, local copies, waits for them, and re-layouts  2.63 us

profile of v4, /device:TPU:1, one launch (start us, length us, event | category | flops | bytes accessed | tf_op | source)
XLA Modules:
  0.0 93.5 jit_solution(17067985305361415878)
XLA Ops:
  0.6 90.3 %shard_map.140 = (bf16[512,4096]{1,0:T(8,128)(2,1)S(1)}, bf16[128,128]{1,0:T(8,128)(2,1)S(1)}) custom-call(bf16[512,4096]{1,0:T(8,128)(2,1)} %bitcast.11, s32[8,8,16]{2,1,0:T(8,128)} %bitcast.13, s32[8,8,16]{2,1,0:T(8,128)} %bitcast.14, bf16[1024,256]{1,0:T(8,128)(2,1)} %bitcast.12, bf16[256,128]{1,0:T(8,128)(2,1)} %dp_hbm.1, ...), custom_call_target="tpu_custom_call" | custom-call | flops 12000000000 | bytes 30000000 | tf_op jit(solution)/shard_map/pallas_call | solution.py:679
  90.9 2.0 %copy.17 = bf16[64,8,4096]{2,1,0:T(8,128)(2,1)} copy(bf16[64,8,4096]{2,1,0:T(8,128)(2,1)S(1)} %bitcast.8) | data formatting | bytes 8388608
  92.9 0.6 copy.18
